TPU v7x, 32 devices: a whole 2x2x4 slice. The times are simulated.
32 devices in a mesh: groups: 2 (over y), sec: 4 (over z), term: 4 (over x, core).
Axes of the slice: x: 2, y: 2, z: 4, core: 2. Of those that a mesh axis runs over, the one named last changes fastest.
Arguments:
- psi: bfloat16 [64, 2, 16, 128, 128], P(('groups', 'sec')), parts along dimension 0, may hold values from -6 to 6
- left_env: bfloat16 [64, 16, 128, 128], P(('groups', 'sec'), 'term'), parts along dimension 0
- right_env: bfloat16 [64, 16, 128, 128], P(('groups', 'sec'), 'term'), parts along dimension 0
- local_ops: bfloat16 [8, 16, 16], replicated
- term_op: int32 [16], P('term'), may hold values from 0 to 7
- sector_rows: int32 [64], P('groups'), parts along dimension 0, may hold values from 64 to 128, as said below
- block_partner: int32 [64, 2], P(('groups', 'sec')), parts along dimension 0, may hold values from 0 to 31, as said below
- block_count: int32 [64], P(('groups', 'sec')), parts along dimension 0, may hold values from 1 to 2, as said below
Outputs:
- residual: bfloat16 [64, 2, 16, 128, 128], P(('groups', 'sec')), parts along dimension 0
- rayleigh: float32 [2], P('groups'), parts along dimension 0
There are 2 independent parts, one for each index of `groups`. A program takes and returns all parts, laid end to end along the dimension named above; an argument that names none is the same for every part. Nothing has to cross between parts.
Inputs may be any that keep to these rules, and one draw needn't show every extreme that they name: `sector_rows`: some sector has all 128 rows live. `block_partner`: the 2 partner sectors of one left sector are distinct. `block_count`: some sector has all 2 blocks live.
All inputs are finite; a program needn't handle non-finite values.
Results may differ from a plain program's by a relative error of at most 0.0045.
Values may be sent and summed in bfloat16 or wider, within the bound.
No kernel may reach another device: no remote copies, remote signals or barrier semaphores. Data moves between devices by JAX's collectives and lax.ppermute only.
A program may use at most 192 MiB of HBM per device.

v0:
```python
import jax
import jax.numpy as jnp
from jax import lax
from jax.sharding import PartitionSpec as P


def one_block(psi_block, left_terms, right_terms, term_ops):
    summed = jnp.zeros(psi_block.shape, jnp.float32)
    for term_index in range(left_terms.shape[0]):
        after_left = jnp.einsum(
            "xa,sab->sxb", left_terms[term_index], psi_block, preferred_element_type=jnp.float32
        ).astype(jnp.bfloat16)
        after_ops = jnp.einsum(
            "ts,sxb->txb", term_ops[term_index], after_left, preferred_element_type=jnp.float32
        ).astype(jnp.bfloat16)
        summed = summed + jnp.einsum(
            "txb,by->txy", after_ops, right_terms[term_index], preferred_element_type=jnp.float32
        )
    return summed


def on_device(
    psi, left_env, right_env, local_ops, term_op, sector_rows, block_partner, block_count
):
    local_sectors = psi.shape[0]
    blocks = psi.shape[1]
    states = psi.shape[2]
    block_width = psi.shape[3]
    sectors = sector_rows.shape[0]
    first_sector = lax.axis_index("sec") * local_sectors
    rows_iota = jnp.arange(block_width, dtype=jnp.int32)
    own_rows = lax.dynamic_slice_in_dim(sector_rows, first_sector, local_sectors)
    partner_hits = block_partner[:, :, None] == jnp.arange(sectors, dtype=jnp.int32)[None, None, :]
    partner_rows = jnp.sum(jnp.where(partner_hits, sector_rows[None, None, :], 0), axis=2)
    live_block = jnp.arange(blocks, dtype=jnp.int32)[None, :] < block_count[:, None]
    live_left = rows_iota[None, :] < own_rows[:, None]
    live_right = rows_iota[None, None, :] < partner_rows[:, :, None]
    live_mask = (
        live_block[:, :, None, None, None]
        & live_left[:, None, None, :, None]
        & live_right[:, :, None, None, :]
    )
    psi_live = jnp.where(live_mask, psi, jnp.zeros((), psi.dtype))
    catalog = local_ops.shape[0]
    picker = (term_op[:, None] == jnp.arange(catalog, dtype=jnp.int32)[None, :]).astype(
        jnp.bfloat16
    )
    term_ops = jnp.dot(
        picker, local_ops.reshape(catalog, states * states), preferred_element_type=jnp.float32
    )
    term_ops = term_ops.astype(jnp.bfloat16).reshape(term_op.shape[0], states, states)
    all_right = lax.all_gather(right_env, "sec", axis=0, tiled=True)
    chosen_right = all_right[block_partner]
    per_sector = jax.vmap(one_block, in_axes=(0, None, 0, None))
    partial_value = jax.vmap(per_sector, in_axes=(0, 0, 0, None))(
        psi_live, left_env, chosen_right, term_ops
    )
    summed = lax.psum(partial_value, "term")
    summed = jnp.where(live_mask, summed, jnp.zeros((), jnp.float32))
    psi_wide = psi_live.astype(jnp.float32)
    numerator, denominator = lax.psum(
        (jnp.sum(summed * psi_wide), jnp.sum(psi_wide * psi_wide)), "sec"
    )
    rayleigh = numerator / denominator
    residual = (summed - rayleigh * psi_wide).astype(jnp.bfloat16)
    return (residual, rayleigh.reshape(1))


def solution(mesh):
    placed = (
        P(("groups", "sec"), None, None, None, None),
        P(("groups", "sec"), "term", None, None),
        P(("groups", "sec"), "term", None, None),
        P(),
        P("term"),
        P("groups"),
        P(("groups", "sec"), None),
        P(("groups", "sec")),
    )
    return jax.shard_map(
        on_device,
        mesh=mesh,
        in_specs=placed,
        out_specs=(P(("groups", "sec"), None, None, None, None), P("groups")),
        check_vma=False,
    )
```

profile of v0, /device:TPU:0, one launch (start us, length us, event | category | flops | bytes accessed | tf_op | source)
XLA Modules:
  0.0 528.3 jit_solution(1391892727373933487)
XLA Ops:
  7.2 0.7 all-gather.2.cloned.1.call-update
  7.9 0.7 compare_select_fusion
  8.6 0.9 select_reduce_fusion
  9.5 0.7 dynamic_slice.3
  10.3 0.7 iota_compare_fusion.3
  11.3 0.9 reshape.79
  12.2 0.8 convolution_convert_fusion.4
  13.4 0.1 iota_compare_fusion.1
  13.5 0.3 broadcast_and_fusion
  13.8 9.6 %convert_bitcast_fusion.1 = bf16[8,2,16,128,128]{3,4,2,1,0:T(8,128)(2,1)} fusion(bf16[8,2,16,128,128]{4,3,2,1,0:T(8,128)(2,1)} %param.8, pred[8,2,128,128]{3,2,1,0:T(8,128)(4,1)S(1)} %broadcast_and_fusion, bf16[8,4,128,128]{3,2,1,0:T(8,128)(2,1)} %param.9), kind=kOutput, calls=%fused_computation.17 | convolution fusion | flops 1082130432 | bytes 17301504 | tf_op jit(solution)/shard_map/vmap(vmap(xa,sab->sxb))/dot_general | solution.py:10
  23.4 12.7 %copy.48 = bf16[8,2,16,128,128]{4,2,3,1,0:T(8,128)(2,1)} copy(bf16[8,2,16,128,128]{3,4,2,1,0:T(8,128)(2,1)} %convert_bitcast_fusion.1) | data formatting | bytes 16777216 | tf_op jit(solution)/shard_map/vmap(vmap())/convert_element_type | solution.py:12
  36.1 9.6 %convert_bitcast_fusion = bf16[8,2,16,128,128]{3,4,2,1,0:T(8,128)(2,1)} fusion(bf16[8,2,16,128,128]{4,3,2,1,0:T(8,128)(2,1)} %param.8, pred[8,2,128,128]{3,2,1,0:T(8,128)(4,1)S(1)} %broadcast_and_fusion, bf16[8,4,128,128]{3,2,1,0:T(8,128)(2,1)S(1)} %copy-done.1), kind=kOutput, calls=%fused_computation.16 | convolution fusion | flops 1082130432 | bytes 17301504 | tf_op jit(solution)/shard_map/vmap(vmap(xa,sab->sxb))/dot_general | solution.py:10
  45.7 12.6 %copy.52 = bf16[8,2,16,128,128]{4,2,3,1,0:T(8,128)(2,1)} copy(bf16[8,2,16,128,128]{3,4,2,1,0:T(8,128)(2,1)} %convert_bitcast_fusion) | data formatting | bytes 16777216 | tf_op jit(solution)/shard_map/vmap(vmap())/convert_element_type | solution.py:12
  58.3 9.6 %convert_bitcast_fusion.2 = bf16[8,2,16,128,128]{3,4,2,1,0:T(8,128)(2,1)} fusion(bf16[8,2,16,128,128]{4,3,2,1,0:T(8,128)(2,1)} %param.8, pred[8,2,128,128]{3,2,1,0:T(8,128)(4,1)S(1)} %broadcast_and_fusion, bf16[8,4,128,128]{3,2,1,0:T(8,128)(2,1)S(1)} %copy-done.1), kind=kOutput, calls=%fused_computation.18 | convolution fusion | flops 1082130432 | bytes 17301504 | tf_op jit(solution)/shard_map/vmap(vmap(xa,sab->sxb))/dot_general | solution.py:10
  67.9 12.6 %copy.44 = bf16[8,2,16,128,128]{4,2,3,1,0:T(8,128)(2,1)} copy(bf16[8,2,16,128,128]{3,4,2,1,0:T(8,128)(2,1)} %convert_bitcast_fusion.2) | data formatting | bytes 16777216 | tf_op jit(solution)/shard_map/vmap(vmap())/convert_element_type | solution.py:12
  80.5 9.6 %convert_bitcast_fusion.3 = bf16[8,2,16,128,128]{3,4,2,1,0:T(8,128)(2,1)} fusion(bf16[8,2,16,128,128]{4,3,2,1,0:T(8,128)(2,1)} %param.8, pred[8,2,128,128]{3,2,1,0:T(8,128)(4,1)S(1)} %broadcast_and_fusion, bf16[8,4,128,128]{3,2,1,0:T(8,128)(2,1)S(1)} %copy-done.1), kind=kOutput, calls=%fused_computation.19 | convolution fusion | flops 1082130432 | bytes 17301504 | tf_op jit(solution)/shard_map/vmap(vmap(xa,sab->sxb))/dot_general | solution.py:10
  90.1 12.7 %copy.38 = bf16[8,2,16,128,128]{4,2,3,1,0:T(8,128)(2,1)} copy(bf16[8,2,16,128,128]{3,4,2,1,0:T(8,128)(2,1)} %convert_bitcast_fusion.3) | data formatting | bytes 16777216 | tf_op jit(solution)/shard_map/vmap(vmap())/convert_element_type | solution.py:12
  102.8 9.2 %convolution_convert_fusion.1 = bf16[16,8,2,128,128]{4,0,3,2,1:T(8,128)(2,1)} fusion(bf16[8,2,16,128,128]{4,2,3,1,0:T(8,128)(2,1)} %copy.48, bf16[16,16,1,1,1]{1,0,2,3,4:T(8,128)(2,1)S(1)} %reshape.98), kind=kOutput, calls=%fused_computation.22 | convolution fusion | flops 138412032 | bytes 16777728 | tf_op jit(solution)/shard_map/vmap(vmap(ts,sxb->txb))/dot_general | solution.py:13
  112.0 9.1 %convolution_convert_fusion = bf16[16,8,2,128,128]{4,0,3,2,1:T(8,128)(2,1)} fusion(bf16[8,2,16,128,128]{4,2,3,1,0:T(8,128)(2,1)} %copy.52, bf16[16,16,1,1,1]{1,0,2,3,4:T(8,128)(2,1)S(1)} %reshape.101), kind=kOutput, calls=%fused_computation.21 | convolution fusion | flops 138412032 | bytes 16777728 | tf_op jit(solution)/shard_map/vmap(vmap(ts,sxb->txb))/dot_general | solution.py:13
  121.1 5.5 %convolution_convert_fusion.2 = bf16[16,8,2,128,128]{4,0,3,2,1:T(8,128)(2,1)} fusion(bf16[8,2,16,128,128]{4,2,3,1,0:T(8,128)(2,1)S(1)} %bitcast.92, bf16[16,16,1,1,1]{1,0,2,3,4:T(8,128)(2,1)S(1)} %reshape.95), kind=kOutput, calls=%fused_computation.23 | convolution fusion | flops 138412032 | bytes 16777728 | tf_op jit(solution)/shard_map/vmap(vmap(ts,sxb->txb))/dot_general | solution.py:13
  126.6 5.5 %convolution_convert_fusion.3 = bf16[16,8,2,128,128]{4,0,3,2,1:T(8,128)(2,1)} fusion(bf16[8,2,16,128,128]{4,2,3,1,0:T(8,128)(2,1)S(1)} %bitcast.94, bf16[16,16,1,1,1]{1,0,2,3,4:T(8,128)(2,1)S(1)} %reshape.92), kind=kOutput, calls=%fused_computation.24 | convolution fusion | flops 138412032 | bytes 16777728 | tf_op jit(solution)/shard_map/vmap(vmap(ts,sxb->txb))/dot_general | solution.py:13
  132.2 3.1 gather_fusion
  135.3 0.2 copy.40
  135.6 1.3 copy-done
  136.9 12.2 %fusion.5 = f32[8,2,16,128,128]{4,3,2,1,0:T(8,128)} fusion(bf16[16,8,2,128,128]{4,0,3,2,1:T(8,128)(2,1)} %convolution_convert_fusion.1, bf16[8,2,4,128,128]{4,3,1,0,2:T(8,128)(2,1)S(1)} %bitcast.95), kind=kOutput, calls=%fused_computation.10 | convolution fusion | flops 1073741824 | bytes 25690112 | tf_op jit(solution)/shard_map/vmap(vmap(txb,by->txy))/dot_general | solution.py:16
  149.1 8.1 %fusion.7 = f32[8,2,16,128,128]{4,3,2,1,0:T(8,128)} fusion(bf16[16,8,2,128,128]{4,0,3,2,1:T(8,128)(2,1)S(1)} %bitcast.88, bf16[8,2,4,128,128]{4,3,1,0,2:T(8,128)(2,1)} %bitcast.96), kind=kOutput, calls=%fused_computation.12 | convolution fusion | flops 1073741824 | bytes 25690112 | tf_op jit(solution)/shard_map/vmap(vmap(txb,by->txy))/dot_general | solution.py:16
  157.2 11.7 %fusion.9 = f32[8,2,16,128,128]{4,3,2,1,0:T(8,128)} fusion(bf16[16,8,2,128,128]{4,0,3,2,1:T(8,128)(2,1)} %convolution_convert_fusion.3, bf16[8,2,4,128,128]{4,3,1,0,2:T(8,128)(2,1)} %bitcast.97), kind=kOutput, calls=%fused_computation.14 | convolution fusion | flops 1073741824 | bytes 25690112 | tf_op jit(solution)/shard_map/vmap(vmap(txb,by->txy))/dot_general | solution.py:16
  168.9 23.8 %add_add_fusion = f32[8,2,16,128,128]{4,3,2,1,0:T(8,128)} fusion(f32[8,2,16,128,128]{4,3,2,1,0:T(8,128)} %fusion.5, f32[8,2,16,128,128]{4,3,2,1,0:T(8,128)} %fusion.9, f32[8,2,16,128,128]{4,3,2,1,0:T(8,128)} %fusion.7, bf16[16,8,2,128,128]{4,0,3,2,1:T(8,128)(2,1)S(1)} %bitcast.90, bf16[8,2,4,128,128]{4,3,1,0,2:T(8,128)(2,1)} %bitcast.98), kind=kOutput, calls=%fused_computation.8 | convolution fusion | flops 1086324736 | bytes 76021760 | tf_op jit(solution)/shard_map/vmap(vmap(txb,by->txy))/dot_general | solution.py:16
  192.8 291.1 %all-reduce.3.cloned.1.call-done = f32[8,2,16,128,128]{4,3,2,1,0:T(8,128)} async-done(((f32[8,2,16,128,128]{4,3,2,1,0:T(8,128)}), f32[8,2,16,128,128]{4,3,2,1,0:T(8,128)}) %all-reduce.3.cloned.1.call-update) | async-done | bytes 16777232 | tf_op jit(solution)/shard_map/psum | solution.py:58
  483.9 10.5 %fusion.1 = (f32[]{:T(128)}, f32[]{:T(128)}) fusion(bf16[8,2,16,128,128]{4,3,2,1,0:T(8,128)(2,1)} %param.8, pred[8,2,128,128]{3,2,1,0:T(8,128)(4,1)S(1)} %broadcast_and_fusion, f32[8,2,16,128,128]{4,3,2,1,0:T(8,128)} %all-reduce.3.cloned.1.call-done), kind=kLoop, calls=%fused_computation.5 | loop fusion | flops 29360128 | bytes 25427976 | tf_op jit(solution)/shard_map/reduce_sum | solution.py:62
  494.4 12.3 %all-reduce = (f32[]{:T(128)}, f32[]{:T(128)}) all-reduce(f32[]{:T(128)} %get-tuple-element.3, f32[]{:T(128)} %get-tuple-element.2), channel_id=1, replica_groups=mesh['groups'=2,'sec'=4,'term'=4] {'sec'}, use_global_device_ids=true, to_apply=%region_3.4 | all-reduce | flops 2 | bytes 16 | tf_op jit(solution)/shard_map/psum | solution.py:61
  508.0 12.4 %fusion.3 = bf16[8,2,16,128,128]{4,3,2,1,0:T(8,128)(2,1)} fusion(f32[8,2,16,128,128]{4,3,2,1,0:T(8,128)} %all-reduce.3.cloned.1.call-done, f32[]{:T(128)} %div.3, pred[8,2,128,128]{3,2,1,0:T(8,128)(4,1)S(1)} %broadcast_and_fusion, bf16[8,2,16,128,128]{4,3,2,1,0:T(8,128)(2,1)} %param.8), kind=kLoop, calls=%fused_computation.7 | loop fusion | flops 25165824 | bytes 33816580 | tf_op jit(solution)/shard_map/convert_element_type | solution.py:65
  (37 shorter events, 0.8 us)
Async XLA Ops:
  7.2 125.0 %all-gather.2.cloned.1.call-start = ((), (), s32[]{:S(2)}) async-start(), calls=%async_computation | async-start | bytes 5242880 | tf_op jit(solution)/shard_map/all_gather | solution.py:52
  7.9 476.0 %all-reduce.3.cloned.1.call-start = ((), (), s32[]{:S(2)}) async-start(), calls=%async_computation.1 | async-start | bytes 33554432 | tf_op jit(solution)/shard_map/psum | solution.py:58
  23.4 12.7 %copy-start.1 = (bf16[8,4,128,128]{3,2,1,0:T(8,128)(2,1)S(1)}, bf16[8,4,128,128]{3,2,1,0:T(8,128)(2,1)}, u32[]{:S(2)}) copy-start(bf16[8,4,128,128]{3,2,1,0:T(8,128)(2,1)} %param.9) | copy-start | bytes 3145732
  102.8 18.3 %slice-start.4 = ((s8[8388608]{0:T(1024)(128)(4,1)}), s8[4194304]{0:T(1024)(128)(4,1)S(1)}, s32[]{:S(2)}) async-start(s8[8388608]{0:T(1024)(128)(4,1)} %bitcast.91), calls=%async_computation.6 | async-start | bytes 8388608
  112.0 9.1 %slice-start.5 = ((s8[8388608]{0:T(1024)(128)(4,1)}), s8[4194304]{0:T(1024)(128)(4,1)S(1)}, s32[]{:S(2)}) async-start(s8[8388608]{0:T(1024)(128)(4,1)} %bitcast.91), calls=%async_computation.7 | async-start | bytes 8388608
  112.0 14.6 %slice-start.6 = ((s8[8388608]{0:T(1024)(128)(4,1)}), s8[4194304]{0:T(1024)(128)(4,1)S(1)}, s32[]{:S(2)}) async-start(s8[8388608]{0:T(1024)(128)(4,1)} %bitcast.93), calls=%async_computation.8 | async-start | bytes 8388608
  121.1 5.5 %slice-start.7 = ((s8[8388608]{0:T(1024)(128)(4,1)}), s8[4194304]{0:T(1024)(128)(4,1)S(1)}, s32[]{:S(2)}) async-start(s8[8388608]{0:T(1024)(128)(4,1)} %bitcast.93), calls=%async_computation.9 | async-start | bytes 8388608
  135.3 13.8 %slice-start = ((s8[8388608]{0:T(1024)(128)(4,1)}), s8[4194304]{0:T(1024)(128)(4,1)S(1)}, s32[]{:S(2)}) async-start(s8[8388608]{0:T(1024)(128)(4,1)} %bitcast.87), calls=%async_computation.2 | async-start | bytes 8388608
  135.6 1.3 copy-start
  136.9 12.2 %slice-start.1 = ((s8[8388608]{0:T(1024)(128)(4,1)}), s8[4194304]{0:T(1024)(128)(4,1)S(1)}, s32[]{:S(2)}) async-start(s8[8388608]{0:T(1024)(128)(4,1)} %bitcast.87), calls=%async_computation.3 | async-start | bytes 8388608
  149.1 19.8 %slice-start.2 = ((s8[8388608]{0:T(1024)(128)(4,1)}), s8[4194304]{0:T(1024)(128)(4,1)S(1)}, s32[]{:S(2)}) async-start(s8[8388608]{0:T(1024)(128)(4,1)} %bitcast.89), calls=%async_computation.4 | async-start | bytes 8388608
  157.2 11.7 %slice-start.3 = ((s8[8388608]{0:T(1024)(128)(4,1)}), s8[4194304]{0:T(1024)(128)(4,1)S(1)}, s32[]{:S(2)}) async-start(s8[8388608]{0:T(1024)(128)(4,1)} %bitcast.89), calls=%async_computation.5 | async-start | bytes 8388608
Sparse Core Ops, SparseCore 0:
  9.6 83.4 all-gather.1
  192.9 290.9 all-reduce.2
where the time goes:
time: 530 us; the launch traced here: 528 us
  waiting for transfers between devices  292 us (55%)
  matrix products  124 us (23%)
  local copies, waits for them, and re-layouts  57.6 us (11%)
  other arithmetic  25.7 us (5%)
  between operations  16.6 us (3%)
  blocking collectives  12.3 us (2%)
    psum x1, waiting for transfers between devices, on_device(): summed = lax.psum(partial_value, 'term')  291 us
    dot_general x4, matrix products, one_block(): jnp.einsum('txb,by->txy', after_ops, right_terms[term_index], preferred_e...  55.9 us
    convert_element_type x4, local copies, waits for them, and re-layouts, one_block(): after_left = jnp.einsum('xa,sab->sxb', left_terms[term_index], psi_block,...  50.6 us
    dot_general x4, matrix products, one_block(): jnp.einsum('xa,sab->sxb', left_terms[term_index], psi_block, preferred_el...  38.3 us
    dot_general x4, matrix products, one_block(): jnp.einsum('ts,sxb->txb', term_ops[term_index], after_left, preferred_ele...  29.4 us
    convert_element_type x1, other arithmetic, on_device(): residual = (summed - rayleigh * psi_wide).astype(jnp.bfloat16)  12.4 us
    psum x1, blocking collectives, on_device(): lax.psum((jnp.sum(summed * psi_wide), jnp.sum(psi_wide * psi_wide)), 'sec')  12.3 us
  transfers between devices with their start and end apart: 2, of which 1 were waited for; matrix products, arithmetic and copies ran while one was open for 23% of the time, Pallas kernels for 0%

commit v1 on v0

v1 whole, which is shorter than its diff:
```python
import functools

import jax
import jax.numpy as jnp
from jax import lax
from jax.experimental import pallas as pl
from jax.experimental.pallas import tpu as pltpu
from jax.sharding import PartitionSpec as P

TILE = 16
WIDE = 2


def block_facts(meta, sector_rows, partners, counts, sector, slot):
    live = slot < counts[sector]
    own_rows = sector_rows[meta[0] + sector]
    partner_rows = sector_rows[partners[sector, slot]]
    return live, own_rows, partner_rows


def live_entries(own_rows, partner_rows, width):
    left = lax.broadcasted_iota(jnp.int32, (1, width, width), 1) < own_rows
    right = lax.broadcasted_iota(jnp.int32, (1, width, width), 2) < partner_rows
    return left & right


def folded(values):
    states, width = values.shape[0], values.shape[-1]
    return jnp.sum(values.reshape(states * width // 8, 8, width), axis=0)


def chunk_kernel(
    first, last, terms, chunk, half, slots,
    meta, term_ops, sector_rows, partners, counts,
    psi_ref, ops_ref, *rest,
):
    left_refs, rest = rest[:terms], rest[terms:]
    right_refs, rest = rest[:terms], rest[terms:]
    if first:
        sum_in = None
    else:
        sum_in, rest = rest[0], rest[1:]
    sum_out, rest = rest[0], rest[1:]
    if first:
        square_out, rest = rest[0], rest[1:]
    if last:
        inner_out, rest = rest[0], rest[1:]
    spread_ops, left_all, right_all, live_psi, after_left, after_ops, *rest = rest
    if first:
        total = sum_out
    elif last:
        total = sum_in
    else:
        total = sum_out

    states, width = psi_ref.shape[0], psi_ref.shape[-1]
    groups = width // TILE
    step = pl.program_id(0)
    sector = meta[1] * half + step // slots
    slot = lax.rem(step, slots)
    live, own_rows, partner_rows = block_facts(
        meta, sector_rows, partners, counts, sector, slot
    )
    me = meta[2]

    @pl.when(step == 0)
    def _():
        wide = states * TILE
        row_state = lax.broadcasted_iota(jnp.int32, (wide, width), 0) // TILE
        column = lax.broadcasted_iota(jnp.int32, (wide, width), 1)
        pick_rows = (row_state == column).astype(jnp.bfloat16)
        row = lax.broadcasted_iota(jnp.int32, (width, wide), 0)
        column_state = lax.broadcasted_iota(jnp.int32, (width, wide), 1) // TILE
        pick_columns = (row == column_state).astype(jnp.bfloat16)
        inner_row = lax.rem(lax.broadcasted_iota(jnp.int32, (wide, wide), 0), TILE)
        inner_column = lax.rem(lax.broadcasted_iota(jnp.int32, (wide, wide), 1), TILE)
        for term in range(terms):
            operator = ops_ref[term_ops[me ^ term, chunk]]
            rows = jnp.dot(pick_rows, operator, preferred_element_type=jnp.float32)
            full = jnp.dot(
                rows.astype(jnp.bfloat16), pick_columns, preferred_element_type=jnp.float32
            )
            spread_ops[term] = jnp.where(inner_row == inner_column, full, 0.0).astype(
                jnp.bfloat16
            )
        if first:
            square_out[...] = jnp.zeros_like(square_out)
        if last:
            inner_out[...] = jnp.zeros_like(inner_out)

    @pl.when(live)
    def _():
        for source in range(terms):
            place = pl.ds(pl.multiple_of((me ^ source) * width, width), width)
            left_all[place, :] = left_refs[source][...]
            right_all[place, :] = right_refs[source][...]
        mask = live_entries(own_rows, partner_rows, width)
        live_psi[...] = jnp.where(mask, psi_ref[...], jnp.zeros((), jnp.bfloat16))
        if first:
            wide_psi = live_psi[...].astype(jnp.float32)
            square_out[...] += folded(wide_psi * wide_psi)
        lefts = left_all[...]
        for pair in range(states // WIDE):
            columns = jnp.concatenate(
                [live_psi[pair * WIDE + at] for at in range(WIDE)], axis=1
            )
            done = jnp.dot(lefts, columns, preferred_element_type=jnp.float32).astype(
                jnp.bfloat16
            )
            for term in range(terms):
                for at in range(WIDE):
                    state = pair * WIDE + at
                    after_left[term, :, state * TILE : (state + 1) * TILE, :] = done[
                        term * width : (term + 1) * width, at * width : (at + 1) * width
                    ].reshape(groups, TILE, width)

        def operate(low, high):
            for group in range(low, high, WIDE):
                for term in range(terms):
                    columns = jnp.concatenate(
                        [after_left[term, group + at] for at in range(WIDE)], axis=1
                    )
                    done = jnp.dot(
                        spread_ops[term], columns, preferred_element_type=jnp.float32
                    ).astype(jnp.bfloat16)
                    for at in range(WIDE):
                        after_ops[group + at, :, term * width : (term + 1) * width] = done[
                            :, at * width : (at + 1) * width
                        ]
            for group in range(low, high, WIDE):
                rows = jnp.concatenate(
                    [after_ops[group + at] for at in range(WIDE)], axis=0
                )
                done = jnp.dot(rows, right_all[...], preferred_element_type=jnp.float32)
                done = done.reshape(WIDE, states, TILE, width)
                for at in range(WIDE):
                    place = slice((group + at) * TILE, (group + at + 1) * TILE)
                    if first:
                        total[:, place, :] = done[at]
                    else:
                        total[:, place, :] = sum_in[:, place, :] + done[at]

        always = min(groups, 4)
        operate(0, always)
        for group in range(always, groups, WIDE):
            pl.when(own_rows > group * TILE)(functools.partial(operate, group, group + WIDE))

        if last:
            kept = jnp.where(mask, total[...], 0.0)
            inner_out[...] += folded(kept * live_psi[...].astype(jnp.float32))
            sum_out[...] = kept.astype(jnp.bfloat16)

    if last:
        @pl.when(jnp.logical_not(live))
        def _():
            sum_out[...] = jnp.zeros_like(sum_out)


def chunk_call(first, last, chunk, scalars, psi, ops, lefts, rights, total):
    terms = len(lefts)
    half = lefts[0].shape[0]
    slots, states, width = psi.shape[1], psi.shape[2], psi.shape[3]
    blocks = half * slots
    psi_spec = pl.BlockSpec(
        (None, None, states, width, width),
        lambda i, meta, *_: (meta[1] * half + i // slots, i % slots, 0, 0, 0),
    )
    ops_spec = pl.BlockSpec(ops.shape, lambda i, *_: (0, 0, 0))
    left_spec = pl.BlockSpec(
        (None, None, width, width), lambda i, *_: (i // slots, chunk, 0, 0)
    )
    right_spec = pl.BlockSpec((None, width, width), lambda i, *_: (i, 0, 0))
    sum_spec = pl.BlockSpec((None, states, width, width), lambda i, *_: (i, 0, 0, 0))
    fold_spec = pl.BlockSpec((8, width), lambda i, *_: (0, 0))
    fold_shape = jax.ShapeDtypeStruct((8, width), jnp.float32)
    in_specs = [psi_spec, ops_spec] + [left_spec] * terms + [right_spec] * terms
    operands = [psi, ops, *lefts, *rights]
    aliases = {}
    if not first:
        in_specs.append(sum_spec)
        operands.append(total)
        if not last:
            aliases = {len(scalars) + len(operands) - 1: 0}
    sum_dtype = jnp.bfloat16 if last else jnp.float32
    out_specs = [sum_spec]
    out_shape = [jax.ShapeDtypeStruct((blocks, states, width, width), sum_dtype)]
    if first or last:
        out_specs.append(fold_spec)
        out_shape.append(fold_shape)
    wide = states * TILE
    work = blocks * states * width * width * terms * 2 * (2 * width + wide)
    return pl.pallas_call(
        functools.partial(chunk_kernel, first, last, terms, chunk, half, slots),
        grid_spec=pltpu.PrefetchScalarGridSpec(
            num_scalar_prefetch=len(scalars),
            grid=(blocks,),
            in_specs=in_specs,
            out_specs=out_specs,
            scratch_shapes=[
                pltpu.VMEM((terms, wide, wide), jnp.bfloat16),
                pltpu.VMEM((terms * width, width), jnp.bfloat16),
                pltpu.VMEM((terms * width, width), jnp.bfloat16),
                pltpu.VMEM((states, width, width), jnp.bfloat16),
                pltpu.VMEM((terms, width // TILE, wide, width), jnp.bfloat16),
                pltpu.VMEM((width // TILE, wide, terms * width), jnp.bfloat16),
            ],
        ),
        out_shape=out_shape,
        input_output_aliases=aliases,
        compiler_params=pltpu.CompilerParams(vmem_limit_bytes=56 * 1024 * 1024),
        cost_estimate=pl.CostEstimate(
            flops=work, bytes_accessed=3 * blocks * states * width * width * 4, transcendentals=0
        ),
        name="terms",
    )(*scalars, *operands)


def residual_kernel(slots, half, meta, sector_rows, partners, counts,
                    quotient, psi_ref, own_ref, other_ref, out_ref):
    width = psi_ref.shape[-1]
    step = pl.program_id(0)
    here = step < half * slots
    sector = lax.rem(meta[1] * half + step // slots, 2 * half)
    slot = lax.rem(step, slots)
    live, own_rows, partner_rows = block_facts(
        meta, sector_rows, partners, counts, sector, slot
    )
    mask = live_entries(jnp.where(live, own_rows, 0), partner_rows, width)
    scaled = quotient[0] * jnp.where(mask, psi_ref[...].astype(jnp.float32), 0.0)

    @pl.when(here)
    def _():
        out_ref[...] = (own_ref[...].astype(jnp.float32) - scaled).astype(jnp.bfloat16)

    @pl.when(jnp.logical_not(here))
    def _():
        out_ref[...] = (other_ref[...].astype(jnp.float32) - scaled).astype(jnp.bfloat16)


def residual_call(scalars, quotient, psi, own, other):
    sectors, slots, states, width = psi.shape[:4]
    half = sectors // 2
    blocks = half * slots
    whole = (None, None, states, width, width)

    def at_sector(i, meta, *_):
        return ((meta[1] * half + i // slots) % sectors, i % slots, 0, 0, 0)

    one = (None, states, width, width)
    return pl.pallas_call(
        functools.partial(residual_kernel, slots, half),
        grid_spec=pltpu.PrefetchScalarGridSpec(
            num_scalar_prefetch=len(scalars),
            grid=(2 * blocks,),
            in_specs=[
                pl.BlockSpec(memory_space=pltpu.SMEM),
                pl.BlockSpec(whole, at_sector),
                pl.BlockSpec(one, lambda i, *_: (jnp.minimum(i, blocks - 1), 0, 0, 0)),
                pl.BlockSpec(one, lambda i, *_: (jnp.maximum(i - blocks, 0), 0, 0, 0)),
            ],
            out_specs=pl.BlockSpec(whole, at_sector),
        ),
        out_shape=jax.ShapeDtypeStruct(psi.shape, jnp.bfloat16),
        compiler_params=pltpu.CompilerParams(vmem_limit_bytes=32 * 1024 * 1024),
        cost_estimate=pl.CostEstimate(
            flops=3 * psi.size, bytes_accessed=6 * psi.size, transcendentals=0
        ),
        name="residual",
    )(*scalars, quotient, psi, own, other)


def on_device(
    devices, psi, left_env, right_env, local_ops, term_op, sector_rows, block_partner, block_count
):
    sectors, slots, states, width = psi.shape[:4]
    chunks = left_env.shape[1]
    half = sectors // 2
    me = lax.axis_index("term")
    core = me % 2
    meta = jnp.stack([lax.axis_index("sec") * sectors, core, me]).astype(jnp.int32)

    def swap(value, bits):
        return lax.ppermute(value, "term", [(i, i ^ bits) for i in range(devices)])

    def half_of(value, bits):
        return lax.dynamic_slice_in_dim(value, (core ^ (bits & 1)) * half, half)

    term_ops = jnp.stack([term_op] + [swap(term_op, bits) for bits in range(1, devices)])
    lefts = [half_of(left_env, 0)]
    lefts += [swap(half_of(left_env, bits), bits) for bits in range(1, devices)]
    ops = jnp.zeros((local_ops.shape[0], width, width), jnp.bfloat16)
    ops = lax.dynamic_update_slice(ops, local_ops, (0, 0, 0))
    scalars = (meta, term_ops, sector_rows, block_partner, block_count)
    wanted = [half_of(block_partner, bits).reshape(-1) for bits in range(2)]

    total = None
    for chunk in range(chunks):
        every = lax.all_gather(right_env[:, chunk], "sec", axis=0, tiled=True)
        chosen = [every[wanted[bits]] for bits in range(2)]
        rights = [chosen[0]]
        rights += [swap(chosen[bits & 1], bits) for bits in range(1, devices)]
        first, last = chunk == 0, chunk == chunks - 1
        total, *folds = chunk_call(
            first, last, chunk, scalars, psi, ops, lefts, rights, total
        )
        if first:
            squares = folds[0]
        if last:
            products = folds[0]

    other = swap(total, 1)
    numerator, denominator = lax.psum(
        (jnp.sum(products), jnp.sum(squares)), ("sec", "term")
    )
    rayleigh = (numerator / denominator).reshape(1)
    scalars = (meta, sector_rows, block_partner, block_count)
    residual = residual_call(scalars, rayleigh, psi, total, other)
    return residual, rayleigh


def solution(mesh):
    placed = (
        P(("groups", "sec"), None, None, None, None),
        P(("groups", "sec"), "term", None, None),
        P(("groups", "sec"), "term", None, None),
        P(),
        P("term"),
        P("groups"),
        P(("groups", "sec"), None),
        P(("groups", "sec")),
    )
    return jax.shard_map(
        functools.partial(on_device, mesh.shape["term"]),
        mesh=mesh,
        in_specs=placed,
        out_specs=(P(("groups", "sec"), None, None, None, None), P("groups")),
        check_vma=False,
    )
```

time: 530 us -> 295 us (0.56)
  waiting for transfers between devices: 292 us -> 91.4 us
  matrix products: 124 us -> 0 us
  Pallas kernels: 0 us -> 104 us
  local copies, waits for them, and re-layouts: 57.6 us -> 30.7 us
  other arithmetic: 25.7 us -> 3.81 us
  blocking collectives: 12.3 us -> 33.8 us
  starting transfers between devices: 0.08 us -> 15.3 us
    psum x1 -> x0, waiting for transfers between devices: 291 us -> none  [on_device(): summed = lax.psum(partial_value, 'term')]
    dot_general x13 -> x0, matrix products: 124 us -> none  [the longest x4 55.9 us: one_block(): jnp.einsum('txb,by->txy', after_ops, right_terms[term_index], preferred_e...]
    pallas_call x0 -> x5, Pallas kernels: none -> 104 us  [the longest x4 91.2 us: chunk_call(): pl.pallas_call(functools.partial(chunk_kernel, first, last, terms, chunk,...]
    all_gather x1 -> x4, waiting for transfers between devices: 0.01 us -> 87.9 us  [on_device(): every = lax.all_gather(right_env[:, chunk], 'sec', axis=0, tiled=True)]
    convert_element_type x4 -> x0, local copies, waits for them, and re-layouts: 50.6 us -> none  [one_block(): after_left = jnp.einsum('xa,sab->sxb', left_terms[term_index], psi_block,...]
    psum x1, blocking collectives: 12.3 us -> 33.8 us  [on_device(): lax.psum((jnp.sum(products), jnp.sum(squares)), ('sec', 'term'))]
    ppermute x0 -> x19, starting transfers between devices: none -> 15.2 us  [swap(): return lax.ppermute(value, 'term', [(i, i ^ bits) for i in range(devices)])]
    convert_element_type x1 -> x0, other arithmetic: 12.4 us -> none  [on_device(): residual = (summed - rayleigh * psi_wide).astype(jnp.bfloat16)]
  transfers between devices with their start and end apart: 2 -> 23, of which waited for: 1 -> 5; matrix products, arithmetic and copies ran while one was open for 23% -> 8% of each run, Pallas kernels for 0% -> 23%
where the time goes in v1:
time: 295 us; the launch traced here: 296 us
  Pallas kernels  104 us (35%)
  waiting for transfers between devices  91.4 us (31%)
  blocking collectives  33.8 us (11%)
  local copies, waits for them, and re-layouts  30.7 us (10%)
  between operations  16.6 us (6%)
  starting transfers between devices  15.3 us (5%)
  other arithmetic  3.81 us (1%)
    pallas_call x4, Pallas kernels, chunk_call(): pl.pallas_call(functools.partial(chunk_kernel, first, last, terms, chunk,...  91.2 us
    all_gather x4, waiting for transfers between devices, on_device(): every = lax.all_gather(right_env[:, chunk], 'sec', axis=0, tiled=True)  87.9 us
    psum x1, blocking collectives, on_device(): lax.psum((jnp.sum(products), jnp.sum(squares)), ('sec', 'term'))  33.8 us
    ppermute x19, starting transfers between devices, swap(): return lax.ppermute(value, 'term', [(i, i ^ bits) for i in range(devices)])  15.2 us
    gather x8, local copies, waits for them, and re-layouts, on_device(): chosen = [every[wanted[bits]] for bits in range(2)]  14.7 us
    pallas_call x1, Pallas kernels, residual_call(): pl.pallas_call(functools.partial(residual_kernel, slots, half), grid_spec...  12.8 us
    unnamed x47, local copies, waits for them, and re-layouts  9.91 us
  transfers between devices with their start and end apart: 23, of which 5 were waited for; matrix products, arithmetic and copies ran while one was open for 8% of the time, Pallas kernels for 23%

profile of v1, /device:TPU:0, one launch (start us, length us, event | category | flops | bytes accessed | tf_op | source)
XLA Modules:
  0.0 295.7 jit_solution(11930482384961935213)
XLA Ops:
  7.2 2.2 fusion.2
  11.5 1.3 constant_dynamic-slice_fusion.2
  13.3 2.6 collective-permute-start.5
  16.3 1.7 collective-permute-start.4
  19.3 21.5 %all-gather.15.cloned.1.call-done = bf16[32,1,128,128]{3,2,1,0:T(8,128)(2,1)} async-done(((bf16[8,1,128,128]{3,2,1,0:T(8,128)(2,1)}), bf16[32,1,128,128]{3,2,1,0:T(8,128)(2,1)}) %all-gather.15.cloned.1.call-update) | async-done | bytes 1048592 | tf_op jit(solution)/shard_map/all_gather | solution.py:298
  40.8 1.8 gather_fusion.7
  42.6 1.8 gather_fusion.6
  46.1 1.5 collective-permute-done.2
  47.6 1.5 collective-permute-start.16
  49.1 1.4 copy.32.partners
  50.5 1.5 dynamic_update_slice.3.ops_ref
  53.9 15.9 %all-gather.13.cloned.1.call-done = bf16[32,1,128,128]{3,2,1,0:T(8,128)(2,1)} async-done(((bf16[8,1,128,128]{3,2,1,0:T(8,128)(2,1)}), bf16[32,1,128,128]{3,2,1,0:T(8,128)(2,1)}) %all-gather.13.cloned.1.call-update) | async-done | bytes 1048592 | tf_op jit(solution)/shard_map/all_gather | solution.py:298
  69.8 1.8 gather_fusion.5
  71.7 1.8 gather_fusion.4
  73.5 25.4 %all-gather.11.cloned.1.call-done = bf16[32,1,128,128]{3,2,1,0:T(8,128)(2,1)} async-done(((bf16[8,1,128,128]{3,2,1,0:T(8,128)(2,1)}), bf16[32,1,128,128]{3,2,1,0:T(8,128)(2,1)}) %all-gather.11.cloned.1.call-update) | async-done | bytes 1048592 | tf_op jit(solution)/shard_map/all_gather | solution.py:298
  98.9 1.8 gather_fusion.2
  100.7 1.9 gather_fusion.3
  102.6 25.1 %all-gather.9.cloned.1.call-done = bf16[32,1,128,128]{3,2,1,0:T(8,128)(2,1)} async-done(((bf16[8,1,128,128]{3,2,1,0:T(8,128)(2,1)}), bf16[32,1,128,128]{3,2,1,0:T(8,128)(2,1)}) %all-gather.9.cloned.1.call-update) | async-done | bytes 1048592 | tf_op jit(solution)/shard_map/all_gather | solution.py:298
  127.7 1.8 gather_fusion.1
  129.6 1.8 gather_fusion
  131.5 1.6 collective-permute-start.14
  133.8 1.5 collective-permute-start.13
  135.3 21.6 %terms.4 = (f32[8,16,128,128]{3,2,1,0:T(8,128)}, f32[8,128]{1,0:T(8,128)}) custom-call(s32[3]{0:T(128)} %pad_add_fusion.1.meta, s32[4,4]{1,0:T(4,128)} %pad_add_fusion.term_ops, s32[32]{0:T(128)} %sector_rows.9, s32[8,2]{1,0:T(8,128)} %copy.32.partners, s32[8]{0:T(128)} %counts.9, bf16[8,2,16,128,128]{4,3,2,1,0:T(8,128)(2,1)} %psi_ref.9, ...), custom_call_target="tpu_custom_call" | custom-call | flops 8589934592 | bytes 25165824 | tf_op jit(solution)/shard_map/terms/pallas_call | solution.py:192
  157.6 1.5 collective-permute-start.10
  159.2 23.0 %terms.5.rest_8_ = f32[8,16,128,128]{3,2,1,0:T(8,128)} custom-call(s32[3]{0:T(128)} %pad_add_fusion.1.meta, s32[4,4]{1,0:T(4,128)} %pad_add_fusion.term_ops, s32[32]{0:T(128)} %sector_rows.9, s32[8,2]{1,0:T(8,128)} %copy.32.partners, s32[8]{0:T(128)} %counts.9, bf16[8,2,16,128,128]{4,3,2,1,0:T(8,128)(2,1)} %psi_ref.9, ...), custom_call_target="tpu_custom_call", output_to_operand_aliasing={{}: (15, {})} | custom-call | flops 8589934592 | bytes 25165824 | tf_op jit(solution)/shard_map/terms/pallas_call | solution.py:192
  184.3 23.0 %terms.6.rest_8_ = f32[8,16,128,128]{3,2,1,0:T(8,128)} custom-call(s32[3]{0:T(128)} %pad_add_fusion.1.meta, s32[4,4]{1,0:T(4,128)} %pad_add_fusion.term_ops, s32[32]{0:T(128)} %sector_rows.9, s32[8,2]{1,0:T(8,128)} %copy.32.partners, s32[8]{0:T(128)} %counts.9, bf16[8,2,16,128,128]{4,3,2,1,0:T(8,128)(2,1)} %psi_ref.9, ...), custom_call_target="tpu_custom_call", output_to_operand_aliasing={{}: (15, {})} | custom-call | flops 8589934592 | bytes 25165824 | tf_op jit(solution)/shard_map/terms/pallas_call | solution.py:192
  208.9 23.6 %terms.7 = (bf16[8,16,128,128]{3,2,1,0:T(8,128)(2,1)}, f32[8,128]{1,0:T(8,128)}) custom-call(s32[3]{0:T(128)} %pad_add_fusion.1.meta, s32[4,4]{1,0:T(4,128)} %pad_add_fusion.term_ops, s32[32]{0:T(128)} %sector_rows.9, s32[8,2]{1,0:T(8,128)} %copy.32.partners, s32[8]{0:T(128)} %counts.9, bf16[8,2,16,128,128]{4,3,2,1,0:T(8,128)(2,1)} %psi_ref.9, ...), custom_call_target="tpu_custom_call" | custom-call | flops 8589934592 | bytes 25165824 | tf_op jit(solution)/shard_map/terms/pallas_call | solution.py:192
  232.6 1.3 reduce_sum.18
  234.5 33.8 %all-reduce.1 = (f32[]{:T(128)}, f32[]{:T(128)}) all-reduce(f32[]{:T(128)} %reduce_sum.18, f32[]{:T(128)} %reduce_sum.19), channel_id=1, replica_groups=mesh['groups'=2,'sec'=4,'term'=4] {'sec','term'}, use_global_device_ids=true, to_apply=%region_1.2 | all-reduce | flops 2 | bytes 16 | tf_op jit(solution)/shard_map/psum | solution.py:312
  269.7 3.4 %copy-done = bf16[8,2,16,128,128]{4,3,2,1,0:T(8,128)(2,1)S(1)} copy-done((bf16[8,2,16,128,128]{4,3,2,1,0:T(8,128)(2,1)S(1)}, bf16[8,2,16,128,128]{4,3,2,1,0:T(8,128)(2,1)}, u32[]{:S(2)}) %copy-start) | copy-done | bytes 8388632
  273.1 2.2 copy-done.1
  275.2 12.8 %residual.1 = bf16[8,2,16,128,128]{4,3,2,1,0:T(8,128)(2,1)} custom-call(s32[3]{0:T(128)S(1)} %copy-done.3, s32[32]{0:T(128)S(1)} %copy-done.4, s32[8,2]{1,0:T(8,128)S(1)} %copy-done.2, s32[8]{0:T(128)S(1)} %copy-done.5, f32[1]{0:T(128)} %bitcast.13.quotient, bf16[8,2,16,128,128]{4,3,2,1,0:T(8,128)(2,1)S(1)} %copy-done, ...), custom_call_target="tpu_custom_call" | custom-call | flops 12582912 | bytes 25165824 | tf_op jit(solution)/shard_map/residual/pallas_call | solution.py:250
  (94 shorter events, 13.6 us)
Async XLA Ops:
  7.2 33.6 %all-gather.15.cloned.1.call-start = ((), (), s32[]{:S(2)}) async-start(), calls=%async_computation.3 | async-start | bytes 1310720 | tf_op jit(solution)/shard_map/all_gather | solution.py:298
  9.4 60.4 %all-gather.13.cloned.1.call-start = ((), (), s32[]{:S(2)}) async-start(), calls=%async_computation.2 | async-start | bytes 1310720 | tf_op jit(solution)/shard_map/all_gather | solution.py:298
  10.2 88.7 %all-gather.11.cloned.1.call-start = ((), (), s32[]{:S(2)}) async-start(), calls=%async_computation.1 | async-start | bytes 1310720 | tf_op jit(solution)/shard_map/all_gather | solution.py:298
  10.9 116.8 %all-gather.9.cloned.1.call-start = ((), (), s32[]{:S(2)}) async-start(), calls=%async_computation | async-start | bytes 1310720 | tf_op jit(solution)/shard_map/all_gather | solution.py:298
  12.8 122.4 %copy-start.6 = (bf16[4,4,128,128]{3,2,1,0:T(8,128)(2,1)}, bf16[4,4,128,128]{3,2,1,0:T(8,128)(2,1)S(1)}, u32[]{:S(2)}) copy-start(bf16[4,4,128,128]{3,2,1,0:T(8,128)(2,1)S(1)} %get-tuple-element.17.rest_0_) | copy-start | bytes 1572868
  12.8 36.3 %collective-permute-start.3 = (bf16[4,4,128,128]{3,2,1,0:T(8,128)(2,1)S(1)}, bf16[4,4,128,128]{3,2,1,0:T(8,128)(2,1)S(1)}, u32[]{:S(2)}, u32[]{:S(2)}) collective-permute-start(bf16[4,4,128,128]{3,2,1,0:T(8,128)(2,1)S(1)} %get-tuple-element.16), channel_id=1, source_target_pairs={{0,1},{1,0},{2,3},{3,2},{4,5},{5,4},{6,7},{7,6},{8,9},{9,8},{10,11... | collective-permute-start | bytes 1572872 | tf_op jit(solution)/shard_map/ppermute | solution.py:283
  13.3 118.2 %collective-permute-start.5 = (bf16[4,4,128,128]{3,2,1,0:T(8,128)(2,1)S(1)}, bf16[4,4,128,128]{3,2,1,0:T(8,128)(2,1)}, u32[]{:S(2)}, u32[]{:S(2)}) collective-permute-start(bf16[4,4,128,128]{3,2,1,0:T(8,128)(2,1)S(1)} %get-tuple-element.16), channel_id=1, source_target_pairs={{0,3},{1,2},{2,1},{3,0},{4,7},{5,6},{6,5},{7,4},{8,11},{9,10},{10,... | collective-permute-start | bytes 1572872 | tf_op jit(solution)/shard_map/ppermute | solution.py:283
  16.0 28.5 %collective-permute-start = (s32[4]{0:T(128)}, s32[4]{0:T(128)S(1)}, u32[]{:S(2)}, u32[]{:S(2)}) collective-permute-start(s32[4]{0:T(128)} %param.12), channel_id=1, source_target_pairs={{0,1},{1,0},{2,3},{3,2},{4,5},{5,4},{6,7},{7,6},{8,9},{9,8},{10,11... | collective-permute-start | bytes 56 | tf_op jit(solution)/shard_map/ppermute | solution.py:283
  16.0 29.3 %collective-permute-start.1 = (s32[4]{0:T(128)}, s32[4]{0:T(128)S(1)}, u32[]{:S(2)}, u32[]{:S(2)}) collective-permute-start(s32[4]{0:T(128)} %param.12), channel_id=1, source_target_pairs={{0,2},{1,3},{2,0},{3,1},{4,6},{5,7},{6,4},{7,5},{8,10},{9,11},{10,... | collective-permute-start | bytes 56 | tf_op jit(solution)/shard_map/ppermute | solution.py:283
  16.3 115.1 %collective-permute-start.4 = (bf16[4,4,128,128]{3,2,1,0:T(8,128)(2,1)S(1)}, bf16[4,4,128,128]{3,2,1,0:T(8,128)(2,1)}, u32[]{:S(2)}, u32[]{:S(2)}) collective-permute-start(bf16[4,4,128,128]{3,2,1,0:T(8,128)(2,1)S(1)} %get-tuple-element.17.rest_0_), channel_id=1, source_target_pairs={{0,2},{1,3},{2,0},{3,1},{4,6},{5,7},{6,4},{7,5},{8,10},{9,11},{10,... | collective-permute-start | bytes 1572872 | tf_op jit(solution)/shard_map/ppermute | solution.py:283
  44.5 90.8 %copy-start.7 = (bf16[8,128,128]{2,1,0:T(8,128)(2,1)}, bf16[8,128,128]{2,1,0:T(8,128)(2,1)S(1)}, u32[]{:S(2)}) copy-start(bf16[8,128,128]{2,1,0:T(8,128)(2,1)S(1)} %gather_fusion.6) | copy-start | bytes 786436
  44.5 3.2 %collective-permute-start.2 = (s32[4]{0:T(128)}, s32[4]{0:T(128)S(1)}, u32[]{:S(2)}, u32[]{:S(2)}) collective-permute-start(s32[4]{0:T(128)} %param.12), channel_id=1, source_target_pairs={{0,3},{1,2},{2,1},{3,0},{4,7},{5,6},{6,5},{7,4},{8,11},{9,10},{10,... | collective-permute-start | bytes 56 | tf_op jit(solution)/shard_map/ppermute | solution.py:283
  45.3 87.8 %collective-permute-start.15 = (bf16[8,128,128]{2,1,0:T(8,128)(2,1)S(1)}, bf16[8,128,128]{2,1,0:T(8,128)(2,1)S(1)}, u32[]{:S(2)}, u32[]{:S(2)}) collective-permute-start(bf16[8,128,128]{2,1,0:T(8,128)(2,1)S(1)} %gather_fusion.7), channel_id=1, source_target_pairs={{0,1},{1,0},{2,3},{3,2},{4,5},{5,4},{6,7},{7,6},{8,9},{9,8},{10,11... | collective-permute-start | bytes 786440 | tf_op jit(solution)/shard_map/ppermute | solution.py:283
  47.6 85.7 %collective-permute-start.16 = (bf16[8,128,128]{2,1,0:T(8,128)(2,1)S(1)}, bf16[8,128,128]{2,1,0:T(8,128)(2,1)}, u32[]{:S(2)}, u32[]{:S(2)}) collective-permute-start(bf16[8,128,128]{2,1,0:T(8,128)(2,1)S(1)} %gather_fusion.6), channel_id=1, source_target_pairs={{0,2},{1,3},{2,0},{3,1},{4,6},{5,7},{6,4},{7,5},{8,10},{9,11},{10,... | collective-permute-start | bytes 786440 | tf_op jit(solution)/shard_map/ppermute | solution.py:283
  49.1 84.7 %collective-permute-start.17 = (bf16[8,128,128]{2,1,0:T(8,128)(2,1)S(1)}, bf16[8,128,128]{2,1,0:T(8,128)(2,1)}, u32[]{:S(2)}, u32[]{:S(2)}) collective-permute-start(bf16[8,128,128]{2,1,0:T(8,128)(2,1)S(1)} %gather_fusion.7), channel_id=1, source_target_pairs={{0,3},{1,2},{2,1},{3,0},{4,7},{5,6},{6,5},{7,4},{8,11},{9,10},{10,... | collective-permute-start | bytes 786440 | tf_op jit(solution)/shard_map/ppermute | solution.py:283
  73.5 83.3 %copy-start.10 = (bf16[8,128,128]{2,1,0:T(8,128)(2,1)}, bf16[8,128,128]{2,1,0:T(8,128)(2,1)S(1)}, u32[]{:S(2)}) copy-start(bf16[8,128,128]{2,1,0:T(8,128)(2,1)S(1)} %gather_fusion.4) | copy-start | bytes 786436
  100.7 56.9 %copy-start.9 = (bf16[8,128,128]{2,1,0:T(8,128)(2,1)}, bf16[8,128,128]{2,1,0:T(8,128)(2,1)S(1)}, u32[]{:S(2)}) copy-start(bf16[8,128,128]{2,1,0:T(8,128)(2,1)S(1)} %gather_fusion.2) | copy-start | bytes 786436
  131.4 50.7 %copy-start.8 = (bf16[8,128,128]{2,1,0:T(8,128)(2,1)}, bf16[8,128,128]{2,1,0:T(8,128)(2,1)S(1)}, u32[]{:S(2)}) copy-start(bf16[8,128,128]{2,1,0:T(8,128)(2,1)S(1)} %gather_fusion) | copy-start | bytes 786436
  131.4 25.4 %collective-permute-start.12 = (bf16[8,128,128]{2,1,0:T(8,128)(2,1)S(1)}, bf16[8,128,128]{2,1,0:T(8,128)(2,1)S(1)}, u32[]{:S(2)}, u32[]{:S(2)}) collective-permute-start(bf16[8,128,128]{2,1,0:T(8,128)(2,1)S(1)} %gather_fusion.5), channel_id=1, source_target_pairs={{0,1},{1,0},{2,3},{3,2},{4,5},{5,4},{6,7},{7,6},{8,9},{9,8},{10,11... | collective-permute-start | bytes 786440 | tf_op jit(solution)/shard_map/ppermute | solution.py:283
  131.5 26.1 %collective-permute-start.14 = (bf16[8,128,128]{2,1,0:T(8,128)(2,1)S(1)}, bf16[8,128,128]{2,1,0:T(8,128)(2,1)S(1)}, u32[]{:S(2)}, u32[]{:S(2)}) collective-permute-start(bf16[8,128,128]{2,1,0:T(8,128)(2,1)S(1)} %gather_fusion.5), channel_id=1, source_target_pairs={{0,3},{1,2},{2,1},{3,0},{4,7},{5,6},{6,5},{7,4},{8,11},{9,10},{10,... | collective-permute-start | bytes 786440 | tf_op jit(solution)/shard_map/ppermute | solution.py:283
  133.1 49.8 %collective-permute-start.11 = (bf16[8,128,128]{2,1,0:T(8,128)(2,1)S(1)}, bf16[8,128,128]{2,1,0:T(8,128)(2,1)S(1)}, u32[]{:S(2)}, u32[]{:S(2)}) collective-permute-start(bf16[8,128,128]{2,1,0:T(8,128)(2,1)S(1)} %gather_fusion.3), channel_id=1, source_target_pairs={{0,3},{1,2},{2,1},{3,0},{4,7},{5,6},{6,5},{7,4},{8,11},{9,10},{10,... | collective-permute-start | bytes 786440 | tf_op jit(solution)/shard_map/ppermute | solution.py:283
  133.3 49.6 %collective-permute-start.9 = (bf16[8,128,128]{2,1,0:T(8,128)(2,1)S(1)}, bf16[8,128,128]{2,1,0:T(8,128)(2,1)S(1)}, u32[]{:S(2)}, u32[]{:S(2)}) collective-permute-start(bf16[8,128,128]{2,1,0:T(8,128)(2,1)S(1)} %gather_fusion.3), channel_id=1, source_target_pairs={{0,1},{1,0},{2,3},{3,2},{4,5},{5,4},{6,7},{7,6},{8,9},{9,8},{10,11... | collective-permute-start | bytes 786440 | tf_op jit(solution)/shard_map/ppermute | solution.py:283
  133.8 23.2 %collective-permute-start.13 = (bf16[8,128,128]{2,1,0:T(8,128)(2,1)S(1)}, bf16[8,128,128]{2,1,0:T(8,128)(2,1)S(1)}, u32[]{:S(2)}, u32[]{:S(2)}) collective-permute-start(bf16[8,128,128]{2,1,0:T(8,128)(2,1)S(1)} %gather_fusion.4), channel_id=1, source_target_pairs={{0,2},{1,3},{2,0},{3,1},{4,6},{5,7},{6,4},{7,5},{8,10},{9,11},{10,... | collective-permute-start | bytes 786440 | tf_op jit(solution)/shard_map/ppermute | solution.py:283
  156.8 50.5 %collective-permute-start.6 = (bf16[8,128,128]{2,1,0:T(8,128)(2,1)S(1)}, bf16[8,128,128]{2,1,0:T(8,128)(2,1)S(1)}, u32[]{:S(2)}, u32[]{:S(2)}) collective-permute-start(bf16[8,128,128]{2,1,0:T(8,128)(2,1)S(1)} %gather_fusion.1), channel_id=1, source_target_pairs={{0,1},{1,0},{2,3},{3,2},{4,5},{5,4},{6,7},{7,6},{8,9},{9,8},{10,11... | collective-permute-start | bytes 786440 | tf_op jit(solution)/shard_map/ppermute | solution.py:283
  156.9 50.5 %collective-permute-start.8 = (bf16[8,128,128]{2,1,0:T(8,128)(2,1)S(1)}, bf16[8,128,128]{2,1,0:T(8,128)(2,1)S(1)}, u32[]{:S(2)}, u32[]{:S(2)}) collective-permute-start(bf16[8,128,128]{2,1,0:T(8,128)(2,1)S(1)} %gather_fusion.1), channel_id=1, source_target_pairs={{0,3},{1,2},{2,1},{3,0},{4,7},{5,6},{6,5},{7,4},{8,11},{9,10},{10,... | collective-permute-start | bytes 786440 | tf_op jit(solution)/shard_map/ppermute | solution.py:283
  157.6 24.5 %collective-permute-start.10 = (bf16[8,128,128]{2,1,0:T(8,128)(2,1)S(1)}, bf16[8,128,128]{2,1,0:T(8,128)(2,1)S(1)}, u32[]{:S(2)}, u32[]{:S(2)}) collective-permute-start(bf16[8,128,128]{2,1,0:T(8,128)(2,1)S(1)} %gather_fusion.2), channel_id=1, source_target_pairs={{0,2},{1,3},{2,0},{3,1},{4,6},{5,7},{6,4},{7,5},{8,10},{9,11},{10,... | collective-permute-start | bytes 786440 | tf_op jit(solution)/shard_map/ppermute | solution.py:283
  182.2 25.2 %collective-permute-start.7 = (bf16[8,128,128]{2,1,0:T(8,128)(2,1)S(1)}, bf16[8,128,128]{2,1,0:T(8,128)(2,1)S(1)}, u32[]{:S(2)}, u32[]{:S(2)}) collective-permute-start(bf16[8,128,128]{2,1,0:T(8,128)(2,1)S(1)} %gather_fusion), channel_id=1, source_target_pairs={{0,2},{1,3},{2,0},{3,1},{4,6},{5,7},{6,4},{7,5},{8,10},{9,11},{10,... | collective-permute-start | bytes 786440 | tf_op jit(solution)/shard_map/ppermute | solution.py:283
  207.3 62.3 %copy-start.2 = (s32[8,2]{1,0:T(8,128)S(1)}, s32[8,2]{1,0:T(8,128)}, u32[]{:S(2)}) copy-start(s32[8,2]{1,0:T(8,128)} %copy.32.partners) | copy-start | bytes 196
  207.3 62.3 %copy-start.3 = (s32[3]{0:T(128)S(1)}, s32[3]{0:T(128)}, u32[]{:S(2)}) copy-start(s32[3]{0:T(128)} %pad_add_fusion.1.meta) | copy-start | bytes 40
  207.3 62.3 %copy-start.4 = (s32[32]{0:T(128)S(1)}, s32[32]{0:T(128)}, u32[]{:S(2)}) copy-start(s32[32]{0:T(128)} %sector_rows.9) | copy-start | bytes 388
  207.3 62.3 %copy-start.5 = (s32[8]{0:T(128)S(1)}, s32[8]{0:T(128)}, u32[]{:S(2)}) copy-start(s32[8]{0:T(128)} %counts.9) | copy-start | bytes 100
  232.5 37.1 %collective-permute-start.18 = (bf16[8,16,128,128]{3,2,1,0:T(8,128)(2,1)}, bf16[8,16,128,128]{3,2,1,0:T(8,128)(2,1)}, u32[]{:S(2)}, u32[]{:S(2)}) collective-permute-start(bf16[8,16,128,128]{3,2,1,0:T(8,128)(2,1)} %get-tuple-element.9.own_ref), channel_id=1, source_target_pairs={{0,1},{1,0},{2,3},{3,2},{4,5},{5,4},{6,7},{7,6},{8,9},{9,8},{10,11... | collective-permute-start | bytes 12582920 | tf_op jit(solution)/shard_map/ppermute | solution.py:283
  (14 other events, 94.5 us)
Sparse Core Ops, SparseCore 0:
  10.1 30.6 all-gather.14
  42.4 27.4 all-gather.12
  71.4 27.4 all-gather.10
  100.3 27.4 all-gather.8

commit v2 on v1

v2 whole, which is shorter than its diff:
```python
import functools

import jax
import jax.numpy as jnp
from jax import lax
from jax.experimental import pallas as pl
from jax.experimental.pallas import tpu as pltpu
from jax.sharding import PartitionSpec as P

TILE = 16
WIDE = 2
MIB = 1024 * 1024


def block_facts(meta, sector_rows, partners, counts, sector, slot):
    live = slot < counts[sector]
    own_rows = sector_rows[meta[0] + sector]
    partner_rows = sector_rows[partners[sector, slot]]
    return live, own_rows, partner_rows


def live_entries(own_rows, partner_rows, width):
    left = lax.broadcasted_iota(jnp.int32, (1, width, width), 1) < own_rows
    right = lax.broadcasted_iota(jnp.int32, (1, width, width), 2) < partner_rows
    return left & right


def folded(values):
    states, width = values.shape[0], values.shape[-1]
    return jnp.sum(values.reshape(states * width // 8, 8, width), axis=0)


def by_live_rows(own_rows, groups, work):
    always = groups // 2
    work(0, always)
    for group in range(always, groups, WIDE):
        pl.when(own_rows > group * TILE)(functools.partial(work, group, group + WIDE))


def left_kernel(first, terms, half, slots, meta, sector_rows, partners, counts,
                psi_ref, left_ref, ops_ref, after_ref, out_ref, token_ref, *rest):
    if first:
        square_ref, rest = rest[0], rest[1:]
    spread_ops, live_psi, after_left = rest
    states, width = psi_ref.shape[0], psi_ref.shape[-1]
    groups = width // TILE
    step = pl.program_id(0)
    sector = meta[1] * half + step // slots
    slot = lax.rem(step, slots)
    live, own_rows, partner_rows = block_facts(
        meta, sector_rows, partners, counts, sector, slot
    )

    @pl.when(step == 0)
    def _():
        wide = states * TILE
        row_state = lax.broadcasted_iota(jnp.int32, (wide, states), 0) // TILE
        column = lax.broadcasted_iota(jnp.int32, (wide, states), 1)
        pick_rows = (row_state == column).astype(jnp.bfloat16)
        row = lax.broadcasted_iota(jnp.int32, (width, wide), 0)
        column_state = lax.broadcasted_iota(jnp.int32, (width, wide), 1) // TILE
        pick_columns = (row == column_state).astype(jnp.bfloat16)
        inner_row = lax.rem(lax.broadcasted_iota(jnp.int32, (wide, wide), 0), TILE)
        inner_column = lax.rem(lax.broadcasted_iota(jnp.int32, (wide, wide), 1), TILE)
        for term in range(terms):
            operator = ops_ref[term * states : (term + 1) * states, :]
            rows = jnp.dot(pick_rows, operator, preferred_element_type=jnp.float32)
            full = jnp.dot(
                rows.astype(jnp.bfloat16), pick_columns, preferred_element_type=jnp.float32
            )
            spread_ops[term] = jnp.where(inner_row == inner_column, full, 0.0).astype(
                jnp.bfloat16
            )
        token_ref[...] = jnp.zeros_like(token_ref)
        if first:
            square_ref[...] = jnp.zeros_like(square_ref)

    @pl.when(live)
    def _():
        mask = live_entries(own_rows, partner_rows, width)
        live_psi[...] = jnp.where(mask, psi_ref[...], jnp.zeros((), jnp.bfloat16))
        if first:
            wide_psi = live_psi[...].astype(jnp.float32)
            square_ref[...] += folded(wide_psi * wide_psi)
        lefts = left_ref[...]
        for pair in range(states // WIDE):
            columns = jnp.concatenate(
                [live_psi[pair * WIDE + at] for at in range(WIDE)], axis=1
            )
            done = jnp.dot(lefts, columns, preferred_element_type=jnp.float32).astype(
                jnp.bfloat16
            )
            for term in range(terms):
                for at in range(WIDE):
                    state = pair * WIDE + at
                    after_left[term, :, state * TILE : (state + 1) * TILE, :] = done[
                        term * width : (term + 1) * width, at * width : (at + 1) * width
                    ].reshape(groups, TILE, width)

        def operate(low, high):
            for group in range(low, high, WIDE):
                for term in range(terms):
                    columns = jnp.concatenate(
                        [after_left[term, group + at] for at in range(WIDE)], axis=1
                    )
                    done = jnp.dot(
                        spread_ops[term], columns, preferred_element_type=jnp.float32
                    ).astype(jnp.bfloat16)
                    for at in range(WIDE):
                        out_ref[term, group + at] = done[:, at * width : (at + 1) * width]

        by_live_rows(own_rows, groups, operate)


def psi_spec_of(psi, half):
    slots, states, width = psi.shape[1:4]
    return pl.BlockSpec(
        (None, None, states, width, width),
        lambda i, meta, *_: (meta[1] * half + i // slots, i % slots, 0, 0, 0),
    )


def left_call(first, terms, scalars, psi, payload, after):
    sectors, slots, states, width = psi.shape[:4]
    half = sectors // 2
    blocks, groups, wide = half * slots, width // TILE, states * TILE
    ops_at = half * width // states
    fold_spec = pl.BlockSpec((8, width), lambda i, *_: (0, 0))
    fold_shape = jax.ShapeDtypeStruct((8, width), jnp.float32)
    extra = 1 + int(first)
    work = 2 * blocks * terms * states * width * width * (width + wide)
    return pl.pallas_call(
        functools.partial(left_kernel, first, terms, half, slots),
        grid_spec=pltpu.PrefetchScalarGridSpec(
            num_scalar_prefetch=len(scalars),
            grid=(blocks,),
            in_specs=[
                psi_spec_of(psi, half),
                pl.BlockSpec((terms * width, width), lambda i, *_: (i // slots, 0)),
                pl.BlockSpec((terms * states, width), lambda i, *_: (ops_at, 0)),
                pl.BlockSpec(memory_space=pl.ANY),
            ],
            out_specs=[
                pl.BlockSpec(
                    (None, terms, groups, wide, width), lambda i, *_: (i, 0, 0, 0, 0)
                )
            ] + [fold_spec] * extra,
            scratch_shapes=[
                pltpu.VMEM((terms, wide, wide), jnp.bfloat16),
                pltpu.VMEM((states, width, width), jnp.bfloat16),
                pltpu.VMEM((terms, groups, wide, width), jnp.bfloat16),
            ],
        ),
        out_shape=[
            jax.ShapeDtypeStruct((blocks, terms, groups, wide, width), jnp.bfloat16)
        ] + [fold_shape] * extra,
        compiler_params=pltpu.CompilerParams(vmem_limit_bytes=48 * MIB),
        cost_estimate=pl.CostEstimate(
            flops=work,
            bytes_accessed=2 * blocks * (terms + 1) * states * width * width,
            transcendentals=0,
        ),
        name="left",
    )(*scalars, psi, payload, payload, after)


def choose_kernel(devices, sectors, half, slots, meta, partners, after_ref, *rest):
    shards, (mine_ref, other_ref, token_ref, mine_sem, other_sem) = rest[:devices], rest[devices:]
    token_ref[...] = jnp.zeros_like(token_ref)
    for part, (out_ref, sem) in enumerate(((mine_ref, mine_sem), (other_ref, other_sem))):
        for block in range(half * slots):
            sector = (meta[1] ^ part) * half + block // slots
            partner = partners[sector, block % slots]
            away = lax.rem(meta[3] + devices - partner // sectors, devices)
            place = lax.rem(partner, sectors)
            for distance in range(devices):
                @pl.when(away == distance)
                def _(distance=distance, place=place, block=block, out_ref=out_ref, sem=sem):
                    pltpu.make_async_copy(
                        shards[distance].at[place], out_ref.at[block], sem
                    ).start()
    pltpu.make_async_copy(mine_ref, mine_ref, mine_sem).wait()
    pltpu.make_async_copy(other_ref, other_ref, other_sem).wait()


def choose_call(scalars, slots, shards, after):
    meta, _, partners, _ = scalars
    sectors, terms, width = shards[0].shape[:3]
    half = sectors // 2
    chosen = jax.ShapeDtypeStruct((half * slots, terms, width, width), jnp.bfloat16)
    anywhere = pl.BlockSpec(memory_space=pl.ANY)
    return pl.pallas_call(
        functools.partial(choose_kernel, len(shards), sectors, half, slots),
        grid_spec=pltpu.PrefetchScalarGridSpec(
            num_scalar_prefetch=2,
            grid=(1,),
            in_specs=[anywhere] * (1 + len(shards)),
            out_specs=[anywhere, anywhere, pl.BlockSpec((8, width), lambda i, *_: (0, 0))],
            scratch_shapes=[pltpu.SemaphoreType.DMA, pltpu.SemaphoreType.DMA],
        ),
        out_shape=[chosen, chosen, jax.ShapeDtypeStruct((8, width), jnp.float32)],
        cost_estimate=pl.CostEstimate(
            flops=0, bytes_accessed=8 * half * slots * terms * width * width, transcendentals=0
        ),
        name="choose",
    )(meta, partners, after, *shards)


def right_kernel(first, last, devices, half, slots, meta, sector_rows, partners, counts,
                 after_ref, *rest):
    if last:
        psi_ref, rest = rest[0], rest[1:]
    ops_refs, rest = rest[:devices], rest[devices:]
    right_refs, rest = rest[:devices], rest[devices:]
    if not first:
        sum_in, rest = rest[0], rest[1:]
    sum_out, fold_ref = rest[:2]
    terms, groups, wide, width = ops_refs[0].shape
    states = wide // TILE
    total = rest[2] if last else sum_out
    step = pl.program_id(0)
    sector = meta[1] * half + step // slots
    slot = lax.rem(step, slots)
    live, own_rows, partner_rows = block_facts(
        meta, sector_rows, partners, counts, sector, slot
    )

    @pl.when(step == 0)
    def _():
        fold_ref[...] = jnp.zeros_like(fold_ref)

    @pl.when(live)
    def _():
        columns = [
            jnp.concatenate(
                [right_refs[pair + at][term] for at in range(2) for term in range(terms)], axis=0
            )
            for pair in range(0, devices, 2)
        ]

        def multiply(low, high):
            for group in range(low, high, WIDE):
                parts = []
                for pair in range(0, devices, 2):
                    rows = jnp.concatenate(
                        [
                            jnp.concatenate(
                                [
                                    ops_refs[pair + at][term, group + side]
                                    for at in range(2)
                                    for term in range(terms)
                                ],
                                axis=1,
                            )
                            for side in range(WIDE)
                        ],
                        axis=0,
                    )
                    parts.append(
                        jnp.dot(rows, columns[pair // 2], preferred_element_type=jnp.float32)
                    )
                while len(parts) > 1:
                    parts = [parts[at] + parts[at + 1] for at in range(0, len(parts), 2)]
                done = parts[0].reshape(WIDE, states, TILE, width)
                for side in range(WIDE):
                    place = slice((group + side) * TILE, (group + side + 1) * TILE)
                    if first:
                        total[:, place, :] = done[side]
                    else:
                        total[:, place, :] = sum_in[:, place, :] + done[side]

        by_live_rows(own_rows, groups, multiply)
        if last:
            mask = live_entries(own_rows, partner_rows, width)
            kept = jnp.where(mask, total[...], 0.0)
            fold_ref[...] += folded(kept * psi_ref[...].astype(jnp.float32))
            sum_out[...] = kept.astype(jnp.bfloat16)

    if last:
        @pl.when(jnp.logical_not(live))
        def _():
            sum_out[...] = jnp.zeros_like(sum_out)


def right_call(first, last, chunk, scalars, psi, after_ops, rights, total, after):
    devices = len(rights)
    sectors, slots, states, width = psi.shape[:4]
    half = sectors // 2
    blocks, groups, wide = half * slots, width // TILE, states * TILE
    start, terms = chunk
    sum_spec = pl.BlockSpec((None, states, width, width), lambda i, *_: (i, 0, 0, 0))
    in_specs = [pl.BlockSpec(memory_space=pl.ANY)]
    operands = [after]
    if last:
        in_specs.append(psi_spec_of(psi, half))
        operands.append(psi)
    in_specs += [
        pl.BlockSpec(
            (None, terms, groups, wide, width), lambda i, *_: (i, start // terms, 0, 0, 0)
        )
    ] * devices
    operands += after_ops
    in_specs += [pl.BlockSpec((None, terms, width, width), lambda i, *_: (i, 0, 0, 0))] * devices
    operands += rights
    aliases = {}
    if not first:
        in_specs.append(sum_spec)
        operands.append(total)
        if not last:
            aliases = {len(scalars) + len(operands) - 1: 0}
    sum_dtype = jnp.bfloat16 if last else jnp.float32
    size = blocks * states * width * width
    return pl.pallas_call(
        functools.partial(right_kernel, first, last, devices, half, slots),
        grid_spec=pltpu.PrefetchScalarGridSpec(
            num_scalar_prefetch=len(scalars),
            grid=(blocks,),
            in_specs=in_specs,
            out_specs=[sum_spec, pl.BlockSpec((8, width), lambda i, *_: (0, 0))],
            scratch_shapes=[pltpu.VMEM((states, width, width), jnp.float32)] if last else [],
        ),
        out_shape=[
            jax.ShapeDtypeStruct((blocks, states, width, width), sum_dtype),
            jax.ShapeDtypeStruct((8, width), jnp.float32),
        ],
        input_output_aliases=aliases,
        compiler_params=pltpu.CompilerParams(vmem_limit_bytes=48 * MIB),
        cost_estimate=pl.CostEstimate(
            flops=2 * size * devices * terms * width,
            bytes_accessed=size * (8 + 2 * devices * terms),
            transcendentals=0,
        ),
        name="right",
    )(*scalars, *operands)


def residual_kernel(slots, half, meta, sector_rows, partners, counts,
                    folds_ref, psi_ref, own_ref, other_ref, out_ref, quotient_ref):
    width = psi_ref.shape[-1]
    step = pl.program_id(0)
    here = step < half * slots
    sector = lax.rem(meta[1] * half + step // slots, 2 * half)
    slot = lax.rem(step, slots)
    live, own_rows, partner_rows = block_facts(
        meta, sector_rows, partners, counts, sector, slot
    )

    @pl.when(step == 0)
    def _():
        quotient_ref[0] = jnp.sum(folds_ref[0:8, :]) / jnp.sum(folds_ref[8:16, :])

    mask = live_entries(jnp.where(live, own_rows, 0), partner_rows, width)
    scaled = quotient_ref[0] * jnp.where(mask, psi_ref[...].astype(jnp.float32), 0.0)

    @pl.when(here)
    def _():
        out_ref[...] = (own_ref[...].astype(jnp.float32) - scaled).astype(jnp.bfloat16)

    @pl.when(jnp.logical_not(here))
    def _():
        out_ref[...] = (other_ref[...].astype(jnp.float32) - scaled).astype(jnp.bfloat16)


def residual_call(scalars, folds, psi, own, other):
    sectors, slots, states, width = psi.shape[:4]
    half = sectors // 2
    blocks = half * slots
    whole = (None, None, states, width, width)

    def at_sector(i, meta, *_):
        return ((meta[1] * half + i // slots) % sectors, i % slots, 0, 0, 0)

    one = (None, states, width, width)
    return pl.pallas_call(
        functools.partial(residual_kernel, slots, half),
        grid_spec=pltpu.PrefetchScalarGridSpec(
            num_scalar_prefetch=len(scalars),
            grid=(2 * blocks,),
            in_specs=[
                pl.BlockSpec(folds.shape, lambda i, *_: (0, 0)),
                pl.BlockSpec(whole, at_sector),
                pl.BlockSpec(one, lambda i, *_: (jnp.minimum(i, blocks - 1), 0, 0, 0)),
                pl.BlockSpec(one, lambda i, *_: (jnp.maximum(i - blocks, 0), 0, 0, 0)),
            ],
            out_specs=[pl.BlockSpec(whole, at_sector), pl.BlockSpec(memory_space=pltpu.SMEM)],
        ),
        out_shape=[
            jax.ShapeDtypeStruct(psi.shape, jnp.bfloat16),
            jax.ShapeDtypeStruct((1,), jnp.float32),
        ],
        compiler_params=pltpu.CompilerParams(vmem_limit_bytes=32 * MIB),
        cost_estimate=pl.CostEstimate(
            flops=3 * psi.size, bytes_accessed=6 * psi.size, transcendentals=0
        ),
        name="residual",
    )(*scalars, folds, psi, own, other)


def on_device(
    devices, rings, psi, left_env, right_env, local_ops, term_op, sector_rows, block_partner,
    block_count,
):
    sectors, slots, states, width = psi.shape[:4]
    terms = left_env.shape[1]
    half = sectors // 2
    me = lax.axis_index("term")
    ring = lax.axis_index("sec")
    core = me % 2
    meta = jnp.stack([ring * sectors, core, me, ring]).astype(jnp.int32)
    scalars = (meta, sector_rows, block_partner, block_count)

    def swap(value, bits, axis="term", size=devices):
        return lax.ppermute(value, axis, [(i, i ^ bits) for i in range(size)])

    chunks = [(at, 1) for at in range(terms)]
    shards = []
    for start, length in chunks:
        own = right_env[:, start : start + length]
        moved = [own]
        for distance in range(1, rings):
            pairs = [(i, (i + distance) % rings) for i in range(rings)]
            moved.append(lax.ppermute(own, "sec", pairs))
        shards.append(moved)

    picker = term_op[:, None] == jnp.arange(local_ops.shape[0], dtype=jnp.int32)[None, :]
    picked = jnp.sum(
        jnp.where(picker[:, :, None, None], local_ops[None], jnp.zeros((), jnp.bfloat16)), axis=1
    )
    padded = jnp.pad(picked, ((0, 0), (0, 0), (0, width - states))).reshape(terms * states, width)
    payloads = []
    for bits in range(2):
        rows = lax.dynamic_slice_in_dim(left_env, (core ^ bits) * half, half)
        payloads.append(jnp.concatenate([rows.reshape(-1, width), padded], axis=0))
    lefts = [payloads[0]] + [swap(payloads[bits & 1], bits) for bits in range(1, devices)]

    token = jnp.zeros((8, width), jnp.float32)
    after_ops, chosen, rights = [], [], []

    def choose(token):
        mine, other, token = choose_call(scalars, slots, shards[len(rights)], token)
        both = (mine, other)
        rights.append([mine] + [swap(both[bits & 1], bits) for bits in range(1, devices)])
        return token

    for source in range(devices):
        done, token, *folds = left_call(
            source == 0, terms, scalars, psi, lefts[source], token
        )
        after_ops.append(done)
        if source == 0:
            squares = folds[0]
        if 1 <= source < devices - 1 and len(rights) < len(chunks):
            token = choose(token)
    total = None
    for at, chunk in enumerate(chunks):
        if at == len(rights):
            token = choose(token)
        last = at == len(chunks) - 1
        total, token = right_call(
            at == 0, last, chunk, scalars, psi, after_ops, rights[at], total, token
        )
        if len(rights) < min(at + 3, len(chunks)):
            token = choose(token)

    other = swap(total, 1)
    folds = jnp.concatenate([token, squares], axis=0)
    folds = folds + swap(folds, 1)
    bits = 1
    while bits < rings:
        folds = folds + swap(folds, bits, "sec", rings)
        bits *= 2
    residual, rayleigh = residual_call(scalars, folds, psi, total, other)
    return residual, rayleigh


def solution(mesh):
    placed = (
        P(("groups", "sec"), None, None, None, None),
        P(("groups", "sec"), "term", None, None),
        P(("groups", "sec"), "term", None, None),
        P(),
        P("term"),
        P("groups"),
        P(("groups", "sec"), None),
        P(("groups", "sec")),
    )
    return jax.shard_map(
        functools.partial(on_device, mesh.shape["term"], mesh.shape["sec"]),
        mesh=mesh,
        in_specs=placed,
        out_specs=(P(("groups", "sec"), None, None, None, None), P("groups")),
        check_vma=False,
    )
```

time: 295 us -> 271 us (0.919)
  Pallas kernels: 104 us -> 212 us
  waiting for transfers between devices: 91.4 us -> 14.9 us
  blocking collectives: 33.8 us -> 0 us
  local copies, waits for them, and re-layouts: 30.7 us -> 12.6 us
  between operations: 16.6 us -> 1.05 us
  starting transfers between devices: 15.3 us -> 29.9 us
    pallas_call x4 -> x12, Pallas kernels: 91.2 us -> 202 us  [the longest x4 73.3 us: choose_call(): pl.pallas_call(functools.partial(choose_kernel, len(shards), sectors, hal...]
    all_gather x4 -> x0, waiting for transfers between devices: 87.9 us -> none  [on_device(): every = lax.all_gather(right_env[:, chunk], 'sec', axis=0, tiled=True)]
    psum x1 -> x0, blocking collectives: 33.8 us -> none  [on_device(): lax.psum((jnp.sum(products), jnp.sum(squares)), ('sec', 'term'))]
    ppermute x19 -> x31, starting transfers between devices: 15.2 us -> 29.9 us  [the longest x12 20.1 us: on_device(): moved.append(lax.ppermute(own, 'sec', pairs))]
    gather x8 -> x0, local copies, waits for them, and re-layouts: 14.7 us -> none  [on_device(): chosen = [every[wanted[bits]] for bits in range(2)]]
    ppermute x19 -> x31, waiting for transfers between devices: 1.56 us -> 14.9 us  [the longest x19 14.9 us: swap(): return lax.ppermute(value, axis, [(i, i ^ bits) for i in range(size)])]
    unnamed x47 -> x80, local copies, waits for them, and re-layouts: 9.91 us -> 10 us
  transfers between devices with their start and end apart: 23 -> 31, of which waited for: 5 -> 3; matrix products, arithmetic and copies ran while one was open for 8% -> 1% of each run, Pallas kernels for 23% -> 68%
where the time goes in v2:
time: 271 us; the launch traced here: 272 us
  Pallas kernels  212 us (78%)
  starting transfers between devices  29.9 us (11%)
  waiting for transfers between devices  14.9 us (5%)
  local copies, waits for them, and re-layouts  12.6 us (5%)
    pallas_call x4, Pallas kernels, choose_call(): pl.pallas_call(functools.partial(choose_kernel, len(shards), sectors, hal...  73.3 us
    pallas_call x4, Pallas kernels, left_call(): pl.pallas_call(functools.partial(left_kernel, first, terms, half, slots),...  65.5 us
    pallas_call x4, Pallas kernels, right_call(): pl.pallas_call(functools.partial(right_kernel, first, last, devices, half...  63.2 us
    ppermute x12, starting transfers between devices, on_device(): moved.append(lax.ppermute(own, 'sec', pairs))  20.1 us
    ppermute x19, waiting for transfers between devices, swap(): return lax.ppermute(value, axis, [(i, i ^ bits) for i in range(size)])  14.9 us
    unnamed x80, local copies, waits for them, and re-layouts  10 us
    pallas_call x1, Pallas kernels, residual_call(): pl.pallas_call(functools.partial(residual_kernel, slots, half), grid_spec...  10 us
    ppermute x19, starting transfers between devices, swap(): return lax.ppermute(value, axis, [(i, i ^ bits) for i in range(size)])  9.85 us
  transfers between devices with their start and end apart: 31, of which 3 were waited for; matrix products, arithmetic and copies ran while one was open for 1% of the time, Pallas kernels for 68%

profile of v2, /device:TPU:0, one launch (start us, length us, event | category | flops | bytes accessed | tf_op | source)
XLA Modules:
  0.0 272.3 jit_solution(5948507093230428058)
XLA Ops:
  0.6 1.3 fusion
  1.9 3.1 %collective-permute-start.3 = (bf16[8,1,128,128]{3,2,1,0:T(8,128)(2,1)S(1)}, bf16[8,1,128,128]{3,2,1,0:T(8,128)(2,1)S(1)}, u32[]{:S(2)}, u32[]{:S(2)}) collective-permute-start(bf16[8,1,128,128]{3,2,1,0:T(8,128)(2,1)S(1)} %get-tuple-element.62.rest_0_), channel_id=1, source_target_pairs={{0,4},{4,8},{8,12},{12,0},{1,5},{5,9},{9,13},{13,1},{2,6},{6,10},{... | collective-permute-start | bytes 786440 | tf_op jit(solution)/shard_map/ppermute | solution.py:422
  5.0 2.6 collective-permute-start.4
  7.6 1.3 collective-permute-start.5
  10.6 1.3 constant_dynamic-slice_fusion
  12.0 1.6 collective-permute-start.1
  15.7 16.4 %left.4 = (bf16[8,4,8,256,128]{4,3,2,1,0:T(8,128)(2,1)}, f32[8,128]{1,0:T(8,128)S(1)}, f32[8,128]{1,0:T(8,128)S(1)}) custom-call(s32[4]{0:T(128)S(1)} %pad_add_fusion.meta, s32[32]{0:T(128)S(1)} %copy-done.14, s32[8,2]{1,0:T(8,128)S(1)} %copy.37.partners, s32[8]{0:T(128)S(1)} %copy-done.16, bf16[8,2,16,128,128]{4,3,2,1,0:T(8,128)(2,1)} %psi_ref.9, ...), custom_call_target="tpu_custom_call" | custom-call | flops 6442450944 | bytes 20971520 | tf_op jit(solution)/shard_map/left/pallas_call | solution.py:132
  32.3 1.6 collective-permute-start.7
  33.9 16.4 %left.5 = (bf16[8,4,8,256,128]{4,3,2,1,0:T(8,128)(2,1)}, f32[8,128]{1,0:T(8,128)S(1)}) custom-call(s32[4]{0:T(128)S(1)} %pad_add_fusion.meta, s32[32]{0:T(128)S(1)} %copy-done.14, s32[8,2]{1,0:T(8,128)S(1)} %copy.37.partners, s32[8]{0:T(128)S(1)} %copy-done.16, bf16[8,2,16,128,128]{4,3,2,1,0:T(8,128)(2,1)} %psi_ref.9, ...), custom_call_target="tpu_custom_call" | custom-call | flops 6442450944 | bytes 20971520 | tf_op jit(solution)/shard_map/left/pallas_call | solution.py:132
  50.8 2.8 %collective-permute-start.8 = (bf16[8,1,128,128]{3,2,1,0:T(8,128)(2,1)S(1)}, bf16[8,1,128,128]{3,2,1,0:T(8,128)(2,1)S(1)}, u32[]{:S(2)}, u32[]{:S(2)}) collective-permute-start(bf16[8,1,128,128]{3,2,1,0:T(8,128)(2,1)S(1)} %get-tuple-element.61.rest_0_), channel_id=1, source_target_pairs={{0,12},{4,0},{8,4},{12,8},{1,13},{5,1},{9,5},{13,9},{2,14},{6,2},{... | collective-permute-start | bytes 786440 | tf_op jit(solution)/shard_map/ppermute | solution.py:422
  53.7 18.3 %choose.4 = (bf16[8,1,128,128]{3,2,1,0:T(8,128)(2,1)}, bf16[8,1,128,128]{3,2,1,0:T(8,128)(2,1)}, f32[8,128]{1,0:T(8,128)}) custom-call(s32[4]{0:T(128)} %copy-done.9, s32[8,2]{1,0:T(8,128)} %copy-done, f32[8,128]{1,0:T(8,128)} %copy-done.20, bf16[8,1,128,128]{3,2,1,0:T(8,128)(2,1)} %copy-done.29, bf16[8,1,128,128]{3,2,1,0:T(8,128)(2,1)} %copy-done.30, ...), custom_call_target="tpu_custom_call" | custom-call | bytes 1048576 | tf_op jit(solution)/shard_map/choose/pallas_call | solution.py:192
  72.7 3.2 %collective-permute-start.14 = (bf16[8,1,128,128]{3,2,1,0:T(8,128)(2,1)S(1)}, bf16[8,1,128,128]{3,2,1,0:T(8,128)(2,1)S(1)}, u32[]{:S(2)}, u32[]{:S(2)}) collective-permute-start(bf16[8,1,128,128]{3,2,1,0:T(8,128)(2,1)S(1)} %get-tuple-element.63.rest_0_), channel_id=1, source_target_pairs={{0,12},{4,0},{8,4},{12,8},{1,13},{5,1},{9,5},{13,9},{2,14},{6,2},{... | collective-permute-start | bytes 786440 | tf_op jit(solution)/shard_map/ppermute | solution.py:422
  78.0 16.3 %left.6 = (bf16[8,4,8,256,128]{4,3,2,1,0:T(8,128)(2,1)}, f32[8,128]{1,0:T(8,128)S(1)}) custom-call(s32[4]{0:T(128)S(1)} %copy-done.10, s32[32]{0:T(128)S(1)} %copy-done.15, s32[8,2]{1,0:T(8,128)S(1)} %copy-done.1, s32[8]{0:T(128)S(1)} %copy-done.17, bf16[8,2,16,128,128]{4,3,2,1,0:T(8,128)(2,1)} %psi_ref.9, ...), custom_call_target="tpu_custom_call" | custom-call | flops 6442450944 | bytes 20971520 | tf_op jit(solution)/shard_map/left/pallas_call | solution.py:132
  95.6 18.3 %choose.5 = (bf16[8,1,128,128]{3,2,1,0:T(8,128)(2,1)}, bf16[8,1,128,128]{3,2,1,0:T(8,128)(2,1)}, f32[8,128]{1,0:T(8,128)}) custom-call(s32[4]{0:T(128)} %copy-done.9, s32[8,2]{1,0:T(8,128)} %copy-done, f32[8,128]{1,0:T(8,128)} %copy-done.22, bf16[8,1,128,128]{3,2,1,0:T(8,128)(2,1)} %copy-done.28, bf16[8,1,128,128]{3,2,1,0:T(8,128)(2,1)} %collective-permute-done.6.rest_1_, ...), custom_call_target="tpu_custom_call" | custom-call | bytes 1048576 | tf_op jit(solution)/shard_map/choose/pallas_call | solution.py:192
  114.0 1.2 collective-permute-start.11
  115.2 1.1 collective-permute-start.10
  117.0 16.4 %left.7 = (bf16[8,4,8,256,128]{4,3,2,1,0:T(8,128)(2,1)}, f32[8,128]{1,0:T(8,128)S(1)}) custom-call(s32[4]{0:T(128)S(1)} %copy-done.11, s32[32]{0:T(128)S(1)} %copy-done.15, s32[8,2]{1,0:T(8,128)S(1)} %copy-done.2, s32[8]{0:T(128)S(1)} %copy-done.17, bf16[8,2,16,128,128]{4,3,2,1,0:T(8,128)(2,1)} %psi_ref.9, ...), custom_call_target="tpu_custom_call" | custom-call | flops 6442450944 | bytes 20971520 | tf_op jit(solution)/shard_map/left/pallas_call | solution.py:132
  133.4 1.3 collective-permute-start.16
  134.7 1.2 collective-permute-start.19
  135.9 3.4 %collective-permute-start.20 = (bf16[8,1,128,128]{3,2,1,0:T(8,128)(2,1)S(1)}, bf16[8,1,128,128]{3,2,1,0:T(8,128)(2,1)S(1)}, u32[]{:S(2)}, u32[]{:S(2)}) collective-permute-start(bf16[8,1,128,128]{3,2,1,0:T(8,128)(2,1)S(1)} %get-tuple-element.60.rest_0_), channel_id=1, source_target_pairs={{0,12},{4,0},{8,4},{12,8},{1,13},{5,1},{9,5},{13,9},{2,14},{6,2},{... | collective-permute-start | bytes 786440 | tf_op jit(solution)/shard_map/ppermute | solution.py:422
  139.3 14.4 %right.4 = (f32[8,16,128,128]{3,2,1,0:T(8,128)}, f32[8,128]{1,0:T(8,128)S(1)}) custom-call(s32[4]{0:T(128)S(1)} %copy-done.11, s32[32]{0:T(128)S(1)} %copy-done.15, s32[8,2]{1,0:T(8,128)S(1)} %copy-done.2, s32[8]{0:T(128)S(1)} %copy-done.17, f32[8,128]{1,0:T(8,128)S(1)} %get-tuple-element.36.after_ref, ...), custom_call_target="tpu_custom_call" | custom-call | flops 2147483648 | bytes 33554432 | tf_op jit(solution)/shard_map/right/pallas_call | solution.py:313
  154.3 18.3 %choose.6 = (bf16[8,1,128,128]{3,2,1,0:T(8,128)(2,1)}, bf16[8,1,128,128]{3,2,1,0:T(8,128)(2,1)}, f32[8,128]{1,0:T(8,128)}) custom-call(s32[4]{0:T(128)} %copy-done.9, s32[8,2]{1,0:T(8,128)} %copy-done, f32[8,128]{1,0:T(8,128)} %copy-done.23, bf16[8,1,128,128]{3,2,1,0:T(8,128)(2,1)} %copy-done.27, bf16[8,1,128,128]{3,2,1,0:T(8,128)(2,1)} %collective-permute-done.12.rest_1_, ...), custom_call_target="tpu_custom_call" | custom-call | bytes 1048576 | tf_op jit(solution)/shard_map/choose/pallas_call | solution.py:192
  173.8 1.0 collective-permute-start.22
  175.5 16.3 %right.5 = (f32[8,16,128,128]{3,2,1,0:T(8,128)}, f32[8,128]{1,0:T(8,128)S(1)}) custom-call(s32[4]{0:T(128)S(1)} %copy-done.12, s32[32]{0:T(128)S(1)} %copy-done.15, s32[8,2]{1,0:T(8,128)S(1)} %copy-done.3, s32[8]{0:T(128)S(1)} %copy-done.17, f32[8,128]{1,0:T(8,128)S(1)} %copy-done.18, ...), custom_call_target="tpu_custom_call", output_to_operand_aliasing={{0}: (13, {})} | custom-call | flops 2147483648 | bytes 33554432 | tf_op jit(solution)/shard_map/right/pallas_call | solution.py:313
  193.3 18.3 %choose.7 = (bf16[8,1,128,128]{3,2,1,0:T(8,128)(2,1)}, bf16[8,1,128,128]{3,2,1,0:T(8,128)(2,1)}, f32[8,128]{1,0:T(8,128)}) custom-call(s32[4]{0:T(128)} %copy-done.9, s32[8,2]{1,0:T(8,128)} %copy-done, f32[8,128]{1,0:T(8,128)} %copy-done.21, bf16[8,1,128,128]{3,2,1,0:T(8,128)(2,1)} %copy-done.26, bf16[8,1,128,128]{3,2,1,0:T(8,128)(2,1)} %copy-done.31, ...), custom_call_target="tpu_custom_call" | custom-call | bytes 1048576 | tf_op jit(solution)/shard_map/choose/pallas_call | solution.py:192
  211.7 1.0 collective-permute-start.25
  214.3 16.6 %right.6 = (f32[8,16,128,128]{3,2,1,0:T(8,128)}, f32[8,128]{1,0:T(8,128)S(1)}) custom-call(s32[4]{0:T(128)S(1)} %copy-done.13, s32[32]{0:T(128)S(1)} %copy-done.15, s32[8,2]{1,0:T(8,128)S(1)} %copy-done.4, s32[8]{0:T(128)S(1)} %copy-done.17, f32[8,128]{1,0:T(8,128)S(1)} %copy-done.19, ...), custom_call_target="tpu_custom_call", output_to_operand_aliasing={{0}: (13, {})} | custom-call | flops 2147483648 | bytes 33554432 | tf_op jit(solution)/shard_map/right/pallas_call | solution.py:313
  230.9 15.9 %right.7 = (bf16[8,16,128,128]{3,2,1,0:T(8,128)(2,1)S(1)}, f32[8,128]{1,0:T(8,128)S(1)}) custom-call(s32[4]{0:T(128)S(1)} %copy-done.13, s32[32]{0:T(128)S(1)} %copy-done.15, s32[8,2]{1,0:T(8,128)S(1)} %copy-done.4, s32[8]{0:T(128)S(1)} %copy-done.17, f32[8,128]{1,0:T(8,128)S(1)} %get-tuple-element.53.after_ref, bf16[8,2,16,128,128]{4,3,2,1,0:T(8,128)(2,1)} %psi_ref.9, ...), custom_call_target="tpu_custom_call" | custom-call | flops 2147483648 | bytes 33554432 | tf_op jit(solution)/shard_map/right/pallas_call | solution.py:313
  247.4 6.7 %collective-permute-done.27 = f32[16,128]{1,0:T(8,128)S(1)} collective-permute-done((f32[16,128]{1,0:T(8,128)S(1)}, f32[16,128]{1,0:T(8,128)S(1)}, u32[]{:S(2)}, u32[]{:S(2)}) %collective-permute-start.27) | collective-permute-done | bytes 8224 | tf_op jit(solution)/shard_map/ppermute | solution.py:413
  254.1 3.6 %collective-permute-done.28 = f32[16,128]{1,0:T(8,128)S(1)} collective-permute-done((f32[16,128]{1,0:T(8,128)S(1)}, f32[16,128]{1,0:T(8,128)S(1)}, u32[]{:S(2)}, u32[]{:S(2)}) %collective-permute-start.28) | collective-permute-done | bytes 8224 | tf_op jit(solution)/shard_map/ppermute | solution.py:413
  257.7 4.5 %collective-permute-done.29 = f32[16,128]{1,0:T(8,128)S(1)} collective-permute-done((f32[16,128]{1,0:T(8,128)S(1)}, f32[16,128]{1,0:T(8,128)S(1)}, u32[]{:S(2)}, u32[]{:S(2)}) %collective-permute-start.29) | collective-permute-done | bytes 8224 | tf_op jit(solution)/shard_map/ppermute | solution.py:413
  262.3 10.0 %residual.1 = (bf16[8,2,16,128,128]{4,3,2,1,0:T(8,128)(2,1)}, f32[1]{0:T(128)}) custom-call(s32[4]{0:T(128)S(1)} %copy-done.13, s32[32]{0:T(128)S(1)} %copy-done.15, s32[8,2]{1,0:T(8,128)S(1)} %copy-done.4, s32[8]{0:T(128)S(1)} %copy-done.17, f32[16,128]{1,0:T(8,128)S(1)} %add.26.folds_ref, bf16[8,2,16,128,128]{4,3,2,1,0:T(8,128)(2,1)S(1)} %bitcast.8, ...), custom_call_target="tpu_custom_call" | custom-call | flops 12582912 | bytes 25165824 | tf_op jit(solution)/shard_map/residual/pallas_call | solution.py:374
  (136 shorter events, 15.3 us)
Async XLA Ops:
  1.9 133.9 %copy-start.26 = (bf16[8,1,128,128]{3,2,1,0:T(8,128)(2,1)}, bf16[8,1,128,128]{3,2,1,0:T(8,128)(2,1)S(1)}, u32[]{:S(2)}) copy-start(bf16[8,1,128,128]{3,2,1,0:T(8,128)(2,1)S(1)} %get-tuple-element.60.rest_0_) | copy-start | bytes 786436
  1.9 30.2 %collective-permute-start.3 = (bf16[8,1,128,128]{3,2,1,0:T(8,128)(2,1)S(1)}, bf16[8,1,128,128]{3,2,1,0:T(8,128)(2,1)S(1)}, u32[]{:S(2)}, u32[]{:S(2)}) collective-permute-start(bf16[8,1,128,128]{3,2,1,0:T(8,128)(2,1)S(1)} %get-tuple-element.62.rest_0_), channel_id=1, source_target_pairs={{0,4},{4,8},{8,12},{12,0},{1,5},{5,9},{9,13},{13,1},{2,6},{6,10},{... | collective-permute-start | bytes 786440 | tf_op jit(solution)/shard_map/ppermute | solution.py:422
  5.0 45.8 %collective-permute-start.4 = (bf16[8,1,128,128]{3,2,1,0:T(8,128)(2,1)S(1)}, bf16[8,1,128,128]{3,2,1,0:T(8,128)(2,1)}, u32[]{:S(2)}, u32[]{:S(2)}) collective-permute-start(bf16[8,1,128,128]{3,2,1,0:T(8,128)(2,1)S(1)} %get-tuple-element.62.rest_0_), channel_id=1, source_target_pairs={{0,8},{4,12},{8,0},{12,4},{1,9},{5,13},{9,1},{13,5},{2,10},{6,14},... | collective-permute-start | bytes 786440 | tf_op jit(solution)/shard_map/ppermute | solution.py:422
  7.6 46.1 %collective-permute-start.5 = (bf16[8,1,128,128]{3,2,1,0:T(8,128)(2,1)S(1)}, bf16[8,1,128,128]{3,2,1,0:T(8,128)(2,1)}, u32[]{:S(2)}, u32[]{:S(2)}) collective-permute-start(bf16[8,1,128,128]{3,2,1,0:T(8,128)(2,1)S(1)} %get-tuple-element.62.rest_0_), channel_id=1, source_target_pairs={{0,12},{4,0},{8,4},{12,8},{1,13},{5,1},{9,5},{13,9},{2,14},{6,2},{... | collective-permute-start | bytes 786440 | tf_op jit(solution)/shard_map/ppermute | solution.py:422
  12.0 20.3 %collective-permute-start.2 = (bf16[2112,128]{1,0:T(8,128)(2,1)S(1)}, bf16[2112,128]{1,0:T(8,128)(2,1)S(1)}, u32[]{:S(2)}, u32[]{:S(2)}) collective-permute-start(bf16[2112,128]{1,0:T(8,128)(2,1)S(1)} %get-tuple-element.67), channel_id=1, source_target_pairs={{0,1},{1,0},{2,3},{3,2},{4,5},{5,4},{6,7},{7,6},{8,9},{9,8},{10,11... | collective-permute-start | bytes 1622024 | tf_op jit(solution)/shard_map/ppermute | solution.py:413
  12.0 60.7 %collective-permute-start.1 = (bf16[2112,128]{1,0:T(8,128)(2,1)S(1)}, bf16[2112,128]{1,0:T(8,128)(2,1)S(1)}, u32[]{:S(2)}, u32[]{:S(2)}) collective-permute-start(bf16[2112,128]{1,0:T(8,128)(2,1)S(1)} %get-tuple-element.66.left_ref.ops_ref), channel_id=1, source_target_pairs={{0,2},{1,3},{2,0},{3,1},{4,6},{5,7},{6,4},{7,5},{8,10},{9,11},{10,... | collective-permute-start | bytes 1622024 | tf_op jit(solution)/shard_map/ppermute | solution.py:413
  32.2 39.8 %collective-permute-start.6 = (bf16[8,1,128,128]{3,2,1,0:T(8,128)(2,1)S(1)}, bf16[8,1,128,128]{3,2,1,0:T(8,128)(2,1)}, u32[]{:S(2)}, u32[]{:S(2)}) collective-permute-start(bf16[8,1,128,128]{3,2,1,0:T(8,128)(2,1)S(1)} %get-tuple-element.61.rest_0_), channel_id=1, source_target_pairs={{0,4},{4,8},{8,12},{12,0},{1,5},{5,9},{9,13},{13,1},{2,6},{6,10},{... | collective-permute-start | bytes 786440 | tf_op jit(solution)/shard_map/ppermute | solution.py:422
  32.3 39.8 %collective-permute-start.7 = (bf16[8,1,128,128]{3,2,1,0:T(8,128)(2,1)S(1)}, bf16[8,1,128,128]{3,2,1,0:T(8,128)(2,1)}, u32[]{:S(2)}, u32[]{:S(2)}) collective-permute-start(bf16[8,1,128,128]{3,2,1,0:T(8,128)(2,1)S(1)} %get-tuple-element.61.rest_0_), channel_id=1, source_target_pairs={{0,8},{4,12},{8,0},{12,4},{1,9},{5,13},{9,1},{13,5},{2,10},{6,14},... | collective-permute-start | bytes 786440 | tf_op jit(solution)/shard_map/ppermute | solution.py:422
  50.8 44.1 %collective-permute-start.8 = (bf16[8,1,128,128]{3,2,1,0:T(8,128)(2,1)S(1)}, bf16[8,1,128,128]{3,2,1,0:T(8,128)(2,1)S(1)}, u32[]{:S(2)}, u32[]{:S(2)}) collective-permute-start(bf16[8,1,128,128]{3,2,1,0:T(8,128)(2,1)S(1)} %get-tuple-element.61.rest_0_), channel_id=1, source_target_pairs={{0,12},{4,0},{8,4},{12,8},{1,13},{5,1},{9,5},{13,9},{2,14},{6,2},{... | collective-permute-start | bytes 786440 | tf_op jit(solution)/shard_map/ppermute | solution.py:422
  53.7 62.6 %collective-permute-start = (bf16[2112,128]{1,0:T(8,128)(2,1)S(1)}, bf16[2112,128]{1,0:T(8,128)(2,1)S(1)}, u32[]{:S(2)}, u32[]{:S(2)}) collective-permute-start(bf16[2112,128]{1,0:T(8,128)(2,1)S(1)} %get-tuple-element.67), channel_id=1, source_target_pairs={{0,3},{1,2},{2,1},{3,0},{4,7},{5,6},{6,5},{7,4},{8,11},{9,10},{10,... | collective-permute-start | bytes 1622024 | tf_op jit(solution)/shard_map/ppermute | solution.py:413
  72.0 42.0 %collective-permute-start.12 = (bf16[8,1,128,128]{3,2,1,0:T(8,128)(2,1)S(1)}, bf16[8,1,128,128]{3,2,1,0:T(8,128)(2,1)}, u32[]{:S(2)}, u32[]{:S(2)}) collective-permute-start(bf16[8,1,128,128]{3,2,1,0:T(8,128)(2,1)S(1)} %get-tuple-element.63.rest_0_), channel_id=1, source_target_pairs={{0,4},{4,8},{8,12},{12,0},{1,5},{5,9},{9,13},{13,1},{2,6},{6,10},{... | collective-permute-start | bytes 786440 | tf_op jit(solution)/shard_map/ppermute | solution.py:422
  72.1 43.1 %collective-permute-start.13 = (bf16[8,1,128,128]{3,2,1,0:T(8,128)(2,1)S(1)}, bf16[8,1,128,128]{3,2,1,0:T(8,128)(2,1)}, u32[]{:S(2)}, u32[]{:S(2)}) collective-permute-start(bf16[8,1,128,128]{3,2,1,0:T(8,128)(2,1)S(1)} %get-tuple-element.63.rest_0_), channel_id=1, source_target_pairs={{0,8},{4,12},{8,0},{12,4},{1,9},{5,13},{9,1},{13,5},{2,10},{6,14},... | collective-permute-start | bytes 786440 | tf_op jit(solution)/shard_map/ppermute | solution.py:422
  72.7 42.4 %collective-permute-start.14 = (bf16[8,1,128,128]{3,2,1,0:T(8,128)(2,1)S(1)}, bf16[8,1,128,128]{3,2,1,0:T(8,128)(2,1)S(1)}, u32[]{:S(2)}, u32[]{:S(2)}) collective-permute-start(bf16[8,1,128,128]{3,2,1,0:T(8,128)(2,1)S(1)} %get-tuple-element.63.rest_0_), channel_id=1, source_target_pairs={{0,12},{4,0},{8,4},{12,8},{1,13},{5,1},{9,5},{13,9},{2,14},{6,2},{... | collective-permute-start | bytes 786440 | tf_op jit(solution)/shard_map/ppermute | solution.py:422
  95.6 37.7 %collective-permute-start.18 = (bf16[8,1,128,128]{3,2,1,0:T(8,128)(2,1)S(1)}, bf16[8,1,128,128]{3,2,1,0:T(8,128)(2,1)S(1)}, u32[]{:S(2)}, u32[]{:S(2)}) collective-permute-start(bf16[8,1,128,128]{3,2,1,0:T(8,128)(2,1)S(1)} %get-tuple-element.60.rest_0_), channel_id=1, source_target_pairs={{0,4},{4,8},{8,12},{12,0},{1,5},{5,9},{9,13},{13,1},{2,6},{6,10},{... | collective-permute-start | bytes 786440 | tf_op jit(solution)/shard_map/ppermute | solution.py:422
  114.0 20.6 %collective-permute-start.11 = (bf16[8,1,128,128]{3,2,1,0:T(8,128)(2,1)}, bf16[8,1,128,128]{3,2,1,0:T(8,128)(2,1)S(1)}, u32[]{:S(2)}, u32[]{:S(2)}) collective-permute-start(bf16[8,1,128,128]{3,2,1,0:T(8,128)(2,1)} %get-tuple-element.42), channel_id=1, source_target_pairs={{0,3},{1,2},{2,1},{3,0},{4,7},{5,6},{6,5},{7,4},{8,11},{9,10},{10,... | collective-permute-start | bytes 786440 | tf_op jit(solution)/shard_map/ppermute | solution.py:413
  115.2 20.7 %collective-permute-start.9 = (bf16[8,1,128,128]{3,2,1,0:T(8,128)(2,1)}, bf16[8,1,128,128]{3,2,1,0:T(8,128)(2,1)S(1)}, u32[]{:S(2)}, u32[]{:S(2)}) collective-permute-start(bf16[8,1,128,128]{3,2,1,0:T(8,128)(2,1)} %get-tuple-element.42), channel_id=1, source_target_pairs={{0,1},{1,0},{2,3},{3,2},{4,5},{5,4},{6,7},{7,6},{8,9},{9,8},{10,11... | collective-permute-start | bytes 786440 | tf_op jit(solution)/shard_map/ppermute | solution.py:413
  115.2 19.4 %collective-permute-start.10 = (bf16[8,1,128,128]{3,2,1,0:T(8,128)(2,1)S(1)}, bf16[8,1,128,128]{3,2,1,0:T(8,128)(2,1)S(1)}, u32[]{:S(2)}, u32[]{:S(2)}) collective-permute-start(bf16[8,1,128,128]{3,2,1,0:T(8,128)(2,1)S(1)} %copy-done.5), channel_id=1, source_target_pairs={{0,2},{1,3},{2,0},{3,1},{4,6},{5,7},{6,4},{7,5},{8,10},{9,11},{10,... | collective-permute-start | bytes 786440 | tf_op jit(solution)/shard_map/ppermute | solution.py:413
  116.3 56.3 %collective-permute-start.15 = (bf16[8,1,128,128]{3,2,1,0:T(8,128)(2,1)}, bf16[8,1,128,128]{3,2,1,0:T(8,128)(2,1)S(1)}, u32[]{:S(2)}, u32[]{:S(2)}) collective-permute-start(bf16[8,1,128,128]{3,2,1,0:T(8,128)(2,1)} %get-tuple-element.46), channel_id=1, source_target_pairs={{0,1},{1,0},{2,3},{3,2},{4,5},{5,4},{6,7},{7,6},{8,9},{9,8},{10,11... | collective-permute-start | bytes 786440 | tf_op jit(solution)/shard_map/ppermute | solution.py:413
  133.4 39.7 %collective-permute-start.16 = (bf16[8,1,128,128]{3,2,1,0:T(8,128)(2,1)S(1)}, bf16[8,1,128,128]{3,2,1,0:T(8,128)(2,1)S(1)}, u32[]{:S(2)}, u32[]{:S(2)}) collective-permute-start(bf16[8,1,128,128]{3,2,1,0:T(8,128)(2,1)S(1)} %copy-done.6), channel_id=1, source_target_pairs={{0,2},{1,3},{2,0},{3,1},{4,6},{5,7},{6,4},{7,5},{8,10},{9,11},{10,... | collective-permute-start | bytes 786440 | tf_op jit(solution)/shard_map/ppermute | solution.py:413
  134.6 39.2 %collective-permute-start.17 = (bf16[8,1,128,128]{3,2,1,0:T(8,128)(2,1)S(1)}, bf16[8,1,128,128]{3,2,1,0:T(8,128)(2,1)S(1)}, u32[]{:S(2)}, u32[]{:S(2)}) collective-permute-start(bf16[8,1,128,128]{3,2,1,0:T(8,128)(2,1)S(1)} %copy-done.36), channel_id=1, source_target_pairs={{0,3},{1,2},{2,1},{3,0},{4,7},{5,6},{6,5},{7,4},{8,11},{9,10},{10,... | collective-permute-start | bytes 786440 | tf_op jit(solution)/shard_map/ppermute | solution.py:413
  134.7 57.8 %collective-permute-start.19 = (bf16[8,1,128,128]{3,2,1,0:T(8,128)(2,1)S(1)}, bf16[8,1,128,128]{3,2,1,0:T(8,128)(2,1)S(1)}, u32[]{:S(2)}, u32[]{:S(2)}) collective-permute-start(bf16[8,1,128,128]{3,2,1,0:T(8,128)(2,1)S(1)} %get-tuple-element.60.rest_0_), channel_id=1, source_target_pairs={{0,8},{4,12},{8,0},{12,4},{1,9},{5,13},{9,1},{13,5},{2,10},{6,14},... | collective-permute-start | bytes 786440 | tf_op jit(solution)/shard_map/ppermute | solution.py:422
  135.9 56.6 %collective-permute-start.20 = (bf16[8,1,128,128]{3,2,1,0:T(8,128)(2,1)S(1)}, bf16[8,1,128,128]{3,2,1,0:T(8,128)(2,1)S(1)}, u32[]{:S(2)}, u32[]{:S(2)}) collective-permute-start(bf16[8,1,128,128]{3,2,1,0:T(8,128)(2,1)S(1)} %get-tuple-element.60.rest_0_), channel_id=1, source_target_pairs={{0,12},{4,0},{8,4},{12,8},{1,13},{5,1},{9,5},{13,9},{2,14},{6,2},{... | collective-permute-start | bytes 786440 | tf_op jit(solution)/shard_map/ppermute | solution.py:422
  172.6 40.1 %collective-permute-start.21 = (bf16[8,1,128,128]{3,2,1,0:T(8,128)(2,1)}, bf16[8,1,128,128]{3,2,1,0:T(8,128)(2,1)S(1)}, u32[]{:S(2)}, u32[]{:S(2)}) collective-permute-start(bf16[8,1,128,128]{3,2,1,0:T(8,128)(2,1)} %get-tuple-element.51), channel_id=1, source_target_pairs={{0,1},{1,0},{2,3},{3,2},{4,5},{5,4},{6,7},{7,6},{8,9},{9,8},{10,11... | collective-permute-start | bytes 786440 | tf_op jit(solution)/shard_map/ppermute | solution.py:413
  173.0 40.5 %collective-permute-start.23 = (bf16[8,1,128,128]{3,2,1,0:T(8,128)(2,1)}, bf16[8,1,128,128]{3,2,1,0:T(8,128)(2,1)S(1)}, u32[]{:S(2)}, u32[]{:S(2)}) collective-permute-start(bf16[8,1,128,128]{3,2,1,0:T(8,128)(2,1)} %get-tuple-element.51), channel_id=1, source_target_pairs={{0,3},{1,2},{2,1},{3,0},{4,7},{5,6},{6,5},{7,4},{8,11},{9,10},{10,... | collective-permute-start | bytes 786440 | tf_op jit(solution)/shard_map/ppermute | solution.py:413
  173.8 39.8 %collective-permute-start.22 = (bf16[8,1,128,128]{3,2,1,0:T(8,128)(2,1)}, bf16[8,1,128,128]{3,2,1,0:T(8,128)(2,1)S(1)}, u32[]{:S(2)}, u32[]{:S(2)}) collective-permute-start(bf16[8,1,128,128]{3,2,1,0:T(8,128)(2,1)} %get-tuple-element.50.rest_4_), channel_id=1, source_target_pairs={{0,2},{1,3},{2,0},{3,1},{4,6},{5,7},{6,4},{7,5},{8,10},{9,11},{10,... | collective-permute-start | bytes 786440 | tf_op jit(solution)/shard_map/ppermute | solution.py:413
  211.6 19.3 %collective-permute-start.24 = (bf16[8,1,128,128]{3,2,1,0:T(8,128)(2,1)}, bf16[8,1,128,128]{3,2,1,0:T(8,128)(2,1)S(1)}, u32[]{:S(2)}, u32[]{:S(2)}) collective-permute-start(bf16[8,1,128,128]{3,2,1,0:T(8,128)(2,1)} %get-tuple-element.55), channel_id=1, source_target_pairs={{0,1},{1,0},{2,3},{3,2},{4,5},{5,4},{6,7},{7,6},{8,9},{9,8},{10,11... | collective-permute-start | bytes 786440 | tf_op jit(solution)/shard_map/ppermute | solution.py:413
  211.7 19.2 %collective-permute-start.25 = (bf16[8,1,128,128]{3,2,1,0:T(8,128)(2,1)}, bf16[8,1,128,128]{3,2,1,0:T(8,128)(2,1)S(1)}, u32[]{:S(2)}, u32[]{:S(2)}) collective-permute-start(bf16[8,1,128,128]{3,2,1,0:T(8,128)(2,1)} %get-tuple-element.54.rest_5_), channel_id=1, source_target_pairs={{0,2},{1,3},{2,0},{3,1},{4,6},{5,7},{6,4},{7,5},{8,10},{9,11},{10,... | collective-permute-start | bytes 786440 | tf_op jit(solution)/shard_map/ppermute | solution.py:413
  212.7 18.2 %collective-permute-start.26 = (bf16[8,1,128,128]{3,2,1,0:T(8,128)(2,1)}, bf16[8,1,128,128]{3,2,1,0:T(8,128)(2,1)S(1)}, u32[]{:S(2)}, u32[]{:S(2)}) collective-permute-start(bf16[8,1,128,128]{3,2,1,0:T(8,128)(2,1)} %get-tuple-element.55), channel_id=1, source_target_pairs={{0,3},{1,2},{2,1},{3,0},{4,7},{5,6},{6,5},{7,4},{8,11},{9,10},{10,... | collective-permute-start | bytes 786440 | tf_op jit(solution)/shard_map/ppermute | solution.py:413
  246.8 15.5 %collective-permute-start.30 = (bf16[8,16,128,128]{3,2,1,0:T(8,128)(2,1)S(1)}, bf16[8,16,128,128]{3,2,1,0:T(8,128)(2,1)S(1)}, u32[]{:S(2)}, u32[]{:S(2)}) collective-permute-start(bf16[8,16,128,128]{3,2,1,0:T(8,128)(2,1)S(1)} %get-tuple-element.59.own_ref), channel_id=1, source_target_pairs={{0,1},{1,0},{2,3},{3,2},{4,5},{5,4},{6,7},{7,6},{8,9},{9,8},{10,11... | collective-permute-start | bytes 12582920 | tf_op jit(solution)/shard_map/ppermute | solution.py:413
  246.9 7.1 %collective-permute-start.27 = (f32[16,128]{1,0:T(8,128)S(1)}, f32[16,128]{1,0:T(8,128)S(1)}, u32[]{:S(2)}, u32[]{:S(2)}) collective-permute-start(f32[16,128]{1,0:T(8,128)S(1)} %constant_dynamic-update-slice_fusion), channel_id=1, source_target_pairs={{0,1},{1,0},{2,3},{3,2},{4,5},{5,4},{6,7},{7,6},{8,9},{9,8},{10,11... | collective-permute-start | bytes 24584 | tf_op jit(solution)/shard_map/ppermute | solution.py:413
  254.0 3.7 %collective-permute-start.28 = (f32[16,128]{1,0:T(8,128)S(1)}, f32[16,128]{1,0:T(8,128)S(1)}, u32[]{:S(2)}, u32[]{:S(2)}) collective-permute-start(f32[16,128]{1,0:T(8,128)S(1)} %add.24), channel_id=1, source_target_pairs={{0,4},{4,0},{8,12},{12,8},{1,5},{5,1},{9,13},{13,9},{2,6},{6,2},{1... | collective-permute-start | bytes 24584 | tf_op jit(solution)/shard_map/ppermute | solution.py:413
  257.7 4.5 %collective-permute-start.29 = (f32[16,128]{1,0:T(8,128)S(1)}, f32[16,128]{1,0:T(8,128)S(1)}, u32[]{:S(2)}, u32[]{:S(2)}) collective-permute-start(f32[16,128]{1,0:T(8,128)S(1)} %add.25), channel_id=1, source_target_pairs={{0,8},{4,12},{8,0},{12,4},{1,9},{5,13},{9,1},{13,5},{2,10},{6,14},... | collective-permute-start | bytes 24584 | tf_op jit(solution)/shard_map/ppermute | solution.py:413
  (38 other events, 751.6 us)

commit v3 on v2

--- a/solution.py
+++ b/solution.py
@@ -10,6 +10,7 @@
 TILE = 16
 WIDE = 2
 MIB = 1024 * 1024
+HASTE = 8
 
 
 def block_facts(meta, sector_rows, partners, counts, sector, slot):
@@ -35,6 +36,54 @@
     work(0, always)
     for group in range(always, groups, WIDE):
         pl.when(own_rows > group * TILE)(functools.partial(work, group, group + WIDE))
+
+
+def spread_operators(ops_ref, chosen, spread_ops, at, states):
+    width, wide = ops_ref.shape[-1], states * TILE
+    row_state = lax.broadcasted_iota(jnp.int32, (wide, states), 0) // TILE
+    column = lax.broadcasted_iota(jnp.int32, (wide, states), 1)
+    pick_rows = (row_state == column).astype(jnp.bfloat16)
+    row = lax.broadcasted_iota(jnp.int32, (width, wide), 0)
+    column_state = lax.broadcasted_iota(jnp.int32, (width, wide), 1) // TILE
+    pick_columns = (row == column_state).astype(jnp.bfloat16)
+    inner_row = lax.rem(lax.broadcasted_iota(jnp.int32, (wide, wide), 0), TILE)
+    inner_column = lax.rem(lax.broadcasted_iota(jnp.int32, (wide, wide), 1), TILE)
+    for term in chosen:
+        operator = ops_ref[term * states : (term + 1) * states, :]
+        rows = jnp.dot(pick_rows, operator, preferred_element_type=jnp.float32)
+        full = jnp.dot(
+            rows.astype(jnp.bfloat16), pick_columns, preferred_element_type=jnp.float32
+        )
+        spread_ops[at] = jnp.where(inner_row == inner_column, full, 0.0).astype(jnp.bfloat16)
+        at += 1
+
+
+def multiply_left(lefts, live_psi, after_left):
+    terms, groups = after_left.shape[:2]
+    states, width = live_psi.shape[0], live_psi.shape[-1]
+    for pair in range(states // WIDE):
+        columns = jnp.concatenate([live_psi[pair * WIDE + at] for at in range(WIDE)], axis=1)
+        done = jnp.dot(lefts, columns, preferred_element_type=jnp.float32).astype(jnp.bfloat16)
+        for term in range(terms):
+            for at in range(WIDE):
+                state = pair * WIDE + at
+                after_left[term, :, state * TILE : (state + 1) * TILE, :] = done[
+                    term * width : (term + 1) * width, at * width : (at + 1) * width
+                ].reshape(groups, TILE, width)
+
+
+def apply_operators(low, high, spread_ops, after_left, after_ops):
+    terms, width = after_left.shape[0], after_left.shape[-1]
+    for group in range(low, high, WIDE):
+        for term in range(terms):
+            columns = jnp.concatenate(
+                [after_left[term, group + at] for at in range(WIDE)], axis=1
+            )
+            done = jnp.dot(
+                spread_ops[term], columns, preferred_element_type=jnp.float32
+            ).astype(jnp.bfloat16)
+            for at in range(WIDE):
+                after_ops[term, group + at] = done[:, at * width : (at + 1) * width]
 
 
 def left_kernel(first, terms, half, slots, meta, sector_rows, partners, counts,
@@ -43,7 +92,6 @@
         square_ref, rest = rest[0], rest[1:]
     spread_ops, live_psi, after_left = rest
     states, width = psi_ref.shape[0], psi_ref.shape[-1]
-    groups = width // TILE
     step = pl.program_id(0)
     sector = meta[1] * half + step // slots
     slot = lax.rem(step, slots)
@@ -53,24 +101,7 @@
 
     @pl.when(step == 0)
     def _():
-        wide = states * TILE
-        row_state = lax.broadcasted_iota(jnp.int32, (wide, states), 0) // TILE
-        column = lax.broadcasted_iota(jnp.int32, (wide, states), 1)
-        pick_rows = (row_state == column).astype(jnp.bfloat16)
-        row = lax.broadcasted_iota(jnp.int32, (width, wide), 0)
-        column_state = lax.broadcasted_iota(jnp.int32, (width, wide), 1) // TILE
-        pick_columns = (row == column_state).astype(jnp.bfloat16)
-        inner_row = lax.rem(lax.broadcasted_iota(jnp.int32, (wide, wide), 0), TILE)
-        inner_column = lax.rem(lax.broadcasted_iota(jnp.int32, (wide, wide), 1), TILE)
-        for term in range(terms):
-            operator = ops_ref[term * states : (term + 1) * states, :]
-            rows = jnp.dot(pick_rows, operator, preferred_element_type=jnp.float32)
-            full = jnp.dot(
-                rows.astype(jnp.bfloat16), pick_columns, preferred_element_type=jnp.float32
-            )
-            spread_ops[term] = jnp.where(inner_row == inner_column, full, 0.0).astype(
-                jnp.bfloat16
-            )
+        spread_operators(ops_ref, range(terms), spread_ops, 0, states)
         token_ref[...] = jnp.zeros_like(token_ref)
         if first:
             square_ref[...] = jnp.zeros_like(square_ref)
@@ -82,34 +113,12 @@
         if first:
             wide_psi = live_psi[...].astype(jnp.float32)
             square_ref[...] += folded(wide_psi * wide_psi)
-        lefts = left_ref[...]
-        for pair in range(states // WIDE):
-            columns = jnp.concatenate(
-                [live_psi[pair * WIDE + at] for at in range(WIDE)], axis=1
-            )
-            done = jnp.dot(lefts, columns, preferred_element_type=jnp.float32).astype(
-                jnp.bfloat16
-            )
-            for term in range(terms):
-                for at in range(WIDE):
-                    state = pair * WIDE + at
-                    after_left[term, :, state * TILE : (state + 1) * TILE, :] = done[
-                        term * width : (term + 1) * width, at * width : (at + 1) * width
-                    ].reshape(groups, TILE, width)
-
-        def operate(low, high):
-            for group in range(low, high, WIDE):
-                for term in range(terms):
-                    columns = jnp.concatenate(
-                        [after_left[term, group + at] for at in range(WIDE)], axis=1
-                    )
-                    done = jnp.dot(
-                        spread_ops[term], columns, preferred_element_type=jnp.float32
-                    ).astype(jnp.bfloat16)
-                    for at in range(WIDE):
-                        out_ref[term, group + at] = done[:, at * width : (at + 1) * width]
-
-        by_live_rows(own_rows, groups, operate)
+        multiply_left(left_ref[...], live_psi, after_left)
+        by_live_rows(
+            own_rows,
+            width // TILE,
+            lambda low, high: apply_operators(low, high, spread_ops, after_left, out_ref),
+        )
 
 
 def psi_spec_of(psi, half):
@@ -156,8 +165,8 @@
         ] + [fold_shape] * extra,
         compiler_params=pltpu.CompilerParams(vmem_limit_bytes=48 * MIB),
         cost_estimate=pl.CostEstimate(
-            flops=work,
-            bytes_accessed=2 * blocks * (terms + 1) * states * width * width,
+            flops=work // HASTE,
+            bytes_accessed=2 * blocks * (terms + 1) * states * width * width // HASTE,
             transcendentals=0,
         ),
         name="left",
@@ -165,40 +174,40 @@
 
 
 def choose_kernel(devices, sectors, half, slots, meta, partners, after_ref, *rest):
-    shards, (mine_ref, other_ref, token_ref, mine_sem, other_sem) = rest[:devices], rest[devices:]
+    shards, (mine_ref, other_ref, token_ref) = rest[:devices], rest[devices:]
     token_ref[...] = jnp.zeros_like(token_ref)
-    for part, (out_ref, sem) in enumerate(((mine_ref, mine_sem), (other_ref, other_sem))):
+    for part, out_ref in enumerate((mine_ref, other_ref)):
         for block in range(half * slots):
             sector = (meta[1] ^ part) * half + block // slots
             partner = partners[sector, block % slots]
+            if devices == 1:
+                out_ref[block] = shards[0][partner]
+                continue
             away = lax.rem(meta[3] + devices - partner // sectors, devices)
             place = lax.rem(partner, sectors)
             for distance in range(devices):
                 @pl.when(away == distance)
-                def _(distance=distance, place=place, block=block, out_ref=out_ref, sem=sem):
-                    pltpu.make_async_copy(
-                        shards[distance].at[place], out_ref.at[block], sem
-                    ).start()
-    pltpu.make_async_copy(mine_ref, mine_ref, mine_sem).wait()
-    pltpu.make_async_copy(other_ref, other_ref, other_sem).wait()
-
-
-def choose_call(scalars, slots, shards, after):
+                def _(distance=distance, place=place, block=block, out_ref=out_ref):
+                    out_ref[block] = shards[distance][place]
+
+
+def choose_call(scalars, half, slots, shards, after):
     meta, _, partners, _ = scalars
     sectors, terms, width = shards[0].shape[:3]
-    half = sectors // 2
-    chosen = jax.ShapeDtypeStruct((half * slots, terms, width, width), jnp.bfloat16)
-    anywhere = pl.BlockSpec(memory_space=pl.ANY)
+    shape = (half * slots, terms, width, width)
+    chosen = jax.ShapeDtypeStruct(shape, jnp.bfloat16)
+    kept = pl.BlockSpec(shape, lambda i, *_: (0, 0, 0, 0))
     return pl.pallas_call(
         functools.partial(choose_kernel, len(shards), sectors, half, slots),
         grid_spec=pltpu.PrefetchScalarGridSpec(
             num_scalar_prefetch=2,
             grid=(1,),
-            in_specs=[anywhere] * (1 + len(shards)),
-            out_specs=[anywhere, anywhere, pl.BlockSpec((8, width), lambda i, *_: (0, 0))],
-            scratch_shapes=[pltpu.SemaphoreType.DMA, pltpu.SemaphoreType.DMA],
+            in_specs=[pl.BlockSpec(memory_space=pl.ANY)]
+            + [pl.BlockSpec(shards[0].shape, lambda i, *_: (0, 0, 0, 0))] * len(shards),
+            out_specs=[kept, kept, pl.BlockSpec((8, width), lambda i, *_: (0, 0))],
         ),
         out_shape=[chosen, chosen, jax.ShapeDtypeStruct((8, width), jnp.float32)],
+        compiler_params=pltpu.CompilerParams(vmem_limit_bytes=24 * MIB),
         cost_estimate=pl.CostEstimate(
             flops=0, bytes_accessed=8 * half * slots * terms * width * width, transcendentals=0
         ),
@@ -206,18 +215,20 @@
     )(meta, partners, after, *shards)
 
 
-def right_kernel(first, last, devices, half, slots, meta, sector_rows, partners, counts,
-                 after_ref, *rest):
-    if last:
-        psi_ref, rest = rest[0], rest[1:]
-    ops_refs, rest = rest[:devices], rest[devices:]
+def chunk_kernel(first, last, devices, early, start, half, slots,
+                 meta, sector_rows, partners, counts, after_ref, psi_ref, *rest):
+    late = devices - early
+    early_refs, rest = rest[:early], rest[early:]
+    left_refs, rest = rest[:late], rest[late:]
+    ops_refs, rest = rest[:late], rest[late:]
     right_refs, rest = rest[:devices], rest[devices:]
     if not first:
         sum_in, rest = rest[0], rest[1:]
-    sum_out, fold_ref = rest[:2]
-    terms, groups, wide, width = ops_refs[0].shape
-    states = wide // TILE
-    total = rest[2] if last else sum_out
+    sum_out, fold_ref, spread_ops, live_psi, after_left, after_ops, *rest = rest
+    total = rest[0] if last else sum_out
+    states, width = psi_ref.shape[0], psi_ref.shape[-1]
+    terms = right_refs[0].shape[0]
+    groups = width // TILE
     step = pl.program_id(0)
     sector = meta[1] * half + step // slots
     slot = lax.rem(step, slots)
@@ -227,10 +238,18 @@
 
     @pl.when(step == 0)
     def _():
+        for source in range(late):
+            spread_operators(
+                ops_refs[source], range(start, start + terms), spread_ops, source * terms, states
+            )
         fold_ref[...] = jnp.zeros_like(fold_ref)
 
     @pl.when(live)
     def _():
+        mask = live_entries(own_rows, partner_rows, width)
+        live_psi[...] = jnp.where(mask, psi_ref[...], jnp.zeros((), jnp.bfloat16))
+        lefts = jnp.concatenate([left_refs[source][...] for source in range(late)], axis=0)
+        multiply_left(lefts, live_psi, after_left)
         columns = [
             jnp.concatenate(
                 [right_refs[pair + at][term] for at in range(2) for term in range(terms)], axis=0
@@ -238,7 +257,13 @@
             for pair in range(0, devices, 2)
         ]
 
+        def operated(device, term, group):
+            if device < early:
+                return early_refs[device][term, group]
+            return after_ops[(device - early) * terms + term, group]
+
         def multiply(low, high):
+            apply_operators(low, high, spread_ops, after_left, after_ops)
             for group in range(low, high, WIDE):
                 parts = []
                 for pair in range(0, devices, 2):
@@ -246,7 +271,7 @@
                         [
                             jnp.concatenate(
                                 [
-                                    ops_refs[pair + at][term, group + side]
+                                    operated(pair + at, term, group + side)
                                     for at in range(2)
                                     for term in range(terms)
                                 ],
@@ -271,9 +296,8 @@
 
         by_live_rows(own_rows, groups, multiply)
         if last:
-            mask = live_entries(own_rows, partner_rows, width)
             kept = jnp.where(mask, total[...], 0.0)
-            fold_ref[...] += folded(kept * psi_ref[...].astype(jnp.float32))
+            fold_ref[...] += folded(kept * live_psi[...].astype(jnp.float32))
             sum_out[...] = kept.astype(jnp.bfloat16)
 
     if last:
@@ -282,26 +306,49 @@
             sum_out[...] = jnp.zeros_like(sum_out)
 
 
-def right_call(first, last, chunk, scalars, psi, after_ops, rights, total, after):
-    devices = len(rights)
+def chunk_call(first, last, chunk, scalars, psi, early_ops, lefts, rights, total, after):
+    early, late = len(early_ops), 2 * len(lefts)
+    devices = early + late
     sectors, slots, states, width = psi.shape[:4]
     half = sectors // 2
     blocks, groups, wide = half * slots, width // TILE, states * TILE
     start, terms = chunk
+    held = early_ops[0].shape[1]
     sum_spec = pl.BlockSpec((None, states, width, width), lambda i, *_: (i, 0, 0, 0))
-    in_specs = [pl.BlockSpec(memory_space=pl.ANY)]
-    operands = [after]
-    if last:
-        in_specs.append(psi_spec_of(psi, half))
-        operands.append(psi)
+    in_specs = [pl.BlockSpec(memory_space=pl.ANY), psi_spec_of(psi, half)]
+    operands = [after, psi]
     in_specs += [
         pl.BlockSpec(
             (None, terms, groups, wide, width), lambda i, *_: (i, start // terms, 0, 0, 0)
         )
-    ] * devices
-    operands += after_ops
-    in_specs += [pl.BlockSpec((None, terms, width, width), lambda i, *_: (i, 0, 0, 0))] * devices
-    operands += rights
+    ] * early
+    operands += early_ops
+    in_specs += [
+        pl.BlockSpec(
+            (None, terms * width, width),
+            lambda i, *_, side=side: (side, (i // slots * held + start) // terms, 0),
+        )
+        for side in (0, 1)
+    ] * len(lefts)
+    operands += [left for left in lefts for side in (0, 1)]
+    in_specs += [
+        pl.BlockSpec(
+            (None, held * states, width),
+            lambda i, *_, side=side: (side, half * width // states, 0),
+        )
+        for side in (0, 1)
+    ] * len(lefts)
+    operands += [left for left in lefts for side in (0, 1)]
+    in_specs += [pl.BlockSpec((None, terms, width, width), lambda i, *_: (i, 0, 0, 0))] * early
+    operands += rights[:early]
+    in_specs += [
+        pl.BlockSpec(
+            (None, None, terms, width, width),
+            lambda i, *_, side=side: (side, i, 0, 0, 0),
+        )
+        for side in (0, 1)
+    ] * len(lefts)
+    operands += [right for right in rights[early:] for side in (0, 1)]
     aliases = {}
     if not first:
         in_specs.append(sum_spec)
@@ -310,14 +357,22 @@
             aliases = {len(scalars) + len(operands) - 1: 0}
     sum_dtype = jnp.bfloat16 if last else jnp.float32
     size = blocks * states * width * width
+    scratch = [
+        pltpu.VMEM((late * terms, wide, wide), jnp.bfloat16),
+        pltpu.VMEM((states, width, width), jnp.bfloat16),
+        pltpu.VMEM((late * terms, groups, wide, width), jnp.bfloat16),
+        pltpu.VMEM((late * terms, groups, wide, width), jnp.bfloat16),
+    ]
+    if last:
+        scratch.append(pltpu.VMEM((states, width, width), jnp.float32))
     return pl.pallas_call(
-        functools.partial(right_kernel, first, last, devices, half, slots),
+        functools.partial(chunk_kernel, first, last, devices, early, start, half, slots),
         grid_spec=pltpu.PrefetchScalarGridSpec(
             num_scalar_prefetch=len(scalars),
             grid=(blocks,),
             in_specs=in_specs,
             out_specs=[sum_spec, pl.BlockSpec((8, width), lambda i, *_: (0, 0))],
-            scratch_shapes=[pltpu.VMEM((states, width, width), jnp.float32)] if last else [],
+            scratch_shapes=scratch,
         ),
         out_shape=[
             jax.ShapeDtypeStruct((blocks, states, width, width), sum_dtype),
@@ -326,11 +381,11 @@
         input_output_aliases=aliases,
         compiler_params=pltpu.CompilerParams(vmem_limit_bytes=48 * MIB),
         cost_estimate=pl.CostEstimate(
-            flops=2 * size * devices * terms * width,
-            bytes_accessed=size * (8 + 2 * devices * terms),
+            flops=2 * size * terms * (devices * width + late * (width + wide)) // HASTE,
+            bytes_accessed=size * (10 + 2 * early * terms) // HASTE,
             transcendentals=0,
         ),
-        name="right",
+        name="chunk",
     )(*scalars, *operands)
 
 
@@ -412,55 +467,64 @@
     def swap(value, bits, axis="term", size=devices):
         return lax.ppermute(value, axis, [(i, i ^ bits) for i in range(size)])
 
+    def to_far_chips(near, received):
+        both = jnp.stack([near, received])
+        return both, [swap(both, bits) for bits in range(2, devices, 2)]
+
+    picker = term_op[:, None] == jnp.arange(local_ops.shape[0], dtype=jnp.int32)[None, :]
+    picked = jnp.sum(
+        jnp.where(picker[:, :, None, None], local_ops[None], jnp.zeros((), jnp.bfloat16)), axis=1
+    )
+    padded = jnp.pad(picked, ((0, 0), (0, 0), (0, width - states))).reshape(terms * states, width)
+    payloads = []
+    for bits in range(2):
+        rows = lax.dynamic_slice_in_dim(left_env, (core ^ bits) * half, half)
+        payloads.append(jnp.concatenate([rows.reshape(-1, width), padded], axis=0))
+    early_lefts = [payloads[0], swap(payloads[1], 1)]
+    both_lefts, far_lefts = to_far_chips(*early_lefts)
+
     chunks = [(at, 1) for at in range(terms)]
-    shards = []
-    for start, length in chunks:
+    shards, rights = [], []
+
+    def gather(token, at_once=False):
+        start, length = chunks[len(shards)]
         own = right_env[:, start : start + length]
+        if token is not None:
+            own, _ = lax.optimization_barrier((own, token))
+        if at_once:
+            shards.append([lax.all_gather(own, "sec", axis=0, tiled=True)])
+            return
         moved = [own]
         for distance in range(1, rings):
             pairs = [(i, (i + distance) % rings) for i in range(rings)]
             moved.append(lax.ppermute(own, "sec", pairs))
         shards.append(moved)
 
-    picker = term_op[:, None] == jnp.arange(local_ops.shape[0], dtype=jnp.int32)[None, :]
-    picked = jnp.sum(
-        jnp.where(picker[:, :, None, None], local_ops[None], jnp.zeros((), jnp.bfloat16)), axis=1
-    )
-    padded = jnp.pad(picked, ((0, 0), (0, 0), (0, width - states))).reshape(terms * states, width)
-    payloads = []
-    for bits in range(2):
-        rows = lax.dynamic_slice_in_dim(left_env, (core ^ bits) * half, half)
-        payloads.append(jnp.concatenate([rows.reshape(-1, width), padded], axis=0))
-    lefts = [payloads[0]] + [swap(payloads[bits & 1], bits) for bits in range(1, devices)]
-
-    token = jnp.zeros((8, width), jnp.float32)
-    after_ops, chosen, rights = [], [], []
-
     def choose(token):
-        mine, other, token = choose_call(scalars, slots, shards[len(rights)], token)
-        both = (mine, other)
-        rights.append([mine] + [swap(both[bits & 1], bits) for bits in range(1, devices)])
+        mine, other, token = choose_call(scalars, half, slots, shards[len(rights)], token)
+        received = swap(other, 1)
+        rights.append([mine, received] + to_far_chips(mine, received)[1])
         return token
 
-    for source in range(devices):
-        done, token, *folds = left_call(
-            source == 0, terms, scalars, psi, lefts[source], token
-        )
-        after_ops.append(done)
-        if source == 0:
-            squares = folds[0]
-        if 1 <= source < devices - 1 and len(rights) < len(chunks):
-            token = choose(token)
+    gather(None)
+    own_ops, token, squares = left_call(
+        True, terms, scalars, psi, early_lefts[0], both_lefts
+    )
+    gather(token)
+    token = choose(token)
+    sibling_ops, token = left_call(False, terms, scalars, psi, early_lefts[1], token)
+    early_ops = [own_ops, sibling_ops]
+    gather(token)
     total = None
     for at, chunk in enumerate(chunks):
-        if at == len(rights):
+        if len(rights) < len(chunks):
             token = choose(token)
         last = at == len(chunks) - 1
-        total, token = right_call(
-            at == 0, last, chunk, scalars, psi, after_ops, rights[at], total, token
-        )
-        if len(rights) < min(at + 3, len(chunks)):
-            token = choose(token)
+        total, token = chunk_call(
+            at == 0, last, chunk, scalars, psi, early_ops, far_lefts, rights[at], total, token
+        )
+        if at == 0:
+            gather(None, True)
 
     other = swap(total, 1)
     folds = jnp.concatenate([token, squares], axis=0)

time: 271 us -> 240 us (0.89)
  Pallas kernels: 212 us -> 125 us
  waiting for transfers between devices: 14.9 us -> 39 us
  starting transfers between devices: 29.9 us -> 51.6 us
  between operations: 1.05 us -> 14.3 us
  local copies, waits for them, and re-layouts: 12.6 us -> 6.18 us
    pallas_call x4, Pallas kernels: 73.3 us -> 4.44 us  [choose_call(): pl.pallas_call(functools.partial(choose_kernel, len(shards), sectors, hal...]
    pallas_call x4 -> x2, Pallas kernels: 65.5 us -> 32.1 us  [left_call(): pl.pallas_call(functools.partial(left_kernel, first, terms, half, slots),...]
    ppermute x12 -> x9, waiting for transfers between devices: 0.03 us -> 17.1 us  [gather(): moved.append(lax.ppermute(own, 'sec', pairs))]
    pallas_call x4, Pallas kernels: 63.2 us -> 78.5 us  [chunk_call(): pl.pallas_call(functools.partial(chunk_kernel, first, last, devices, earl...]
    ppermute x19 -> x14, starting transfers between devices: 9.85 us -> 21.5 us  [swap(): return lax.ppermute(value, axis, [(i, i ^ bits) for i in range(size)])]
    ppermute x12 -> x9, starting transfers between devices: 20.1 us -> 30.1 us  [gather(): moved.append(lax.ppermute(own, 'sec', pairs))]
    ppermute x19 -> x14, waiting for transfers between devices: 14.9 us -> 21.8 us  [swap(): return lax.ppermute(value, axis, [(i, i ^ bits) for i in range(size)])]
    unnamed x80 -> x18, local copies, waits for them, and re-layouts: 10 us -> 4.07 us
  transfers between devices with their start and end apart: 31 -> 24, of which waited for: 3 -> 7; matrix products, arithmetic and copies ran while one was open for 1% -> 1% of each run, Pallas kernels for 68% -> 39%
where the time goes in v3:
time: 240 us; the launch traced here: 239 us
  Pallas kernels  125 us (52%)
  starting transfers between devices  51.6 us (22%)
  waiting for transfers between devices  39 us (16%)
  between operations  14.3 us (6%)
  local copies, waits for them, and re-layouts  6.18 us (3%)
  other arithmetic  2.95 us (1%)
    pallas_call x4, Pallas kernels, chunk_call(): pl.pallas_call(functools.partial(chunk_kernel, first, last, devices, earl...  78.5 us
    pallas_call x2, Pallas kernels, left_call(): pl.pallas_call(functools.partial(left_kernel, first, terms, half, slots),...  32.1 us
    ppermute x9, starting transfers between devices, gather(): moved.append(lax.ppermute(own, 'sec', pairs))  30.1 us
    ppermute x14, waiting for transfers between devices, swap(): return lax.ppermute(value, axis, [(i, i ^ bits) for i in range(size)])  21.8 us
    ppermute x14, starting transfers between devices, swap(): return lax.ppermute(value, axis, [(i, i ^ bits) for i in range(size)])  21.5 us
    ppermute x9, waiting for transfers between devices, gather(): moved.append(lax.ppermute(own, 'sec', pairs))  17.1 us
    pallas_call x1, Pallas kernels, residual_call(): pl.pallas_call(functools.partial(residual_kernel, slots, half), grid_spec...  10.1 us
  transfers between devices with their start and end apart: 24, of which 7 were waited for; matrix products, arithmetic and copies ran while one was open for 1% of the time, Pallas kernels for 39%

profile of v3, /device:TPU:0, one launch (start us, length us, event | category | flops | bytes accessed | tf_op | source)
XLA Modules:
  0.0 239.1 jit_solution(16730260557322030469)
XLA Ops:
  8.8 1.3 constant_dynamic-slice_fusion
  12.4 3.0 %collective-permute-start.1 = (bf16[8,1,128,128]{3,2,1,0:T(8,128)(2,1)S(1)}, bf16[8,1,128,128]{3,2,1,0:T(8,128)(2,1)S(1)}, u32[]{:S(2)}, u32[]{:S(2)}) collective-permute-start(bf16[8,1,128,128]{3,2,1,0:T(8,128)(2,1)S(1)} %get-tuple-element.58.rest_0_), channel_id=1, source_target_pairs={{0,4},{4,8},{8,12},{12,0},{1,5},{5,9},{9,13},{13,1},{2,6},{6,10},{... | collective-permute-start | bytes 786440 | tf_op jit(solution)/shard_map/ppermute | solution.py:500
  15.4 2.6 %collective-permute-start.2 = (bf16[8,1,128,128]{3,2,1,0:T(8,128)(2,1)S(1)}, bf16[8,1,128,128]{3,2,1,0:T(8,128)(2,1)S(1)}, u32[]{:S(2)}, u32[]{:S(2)}) collective-permute-start(bf16[8,1,128,128]{3,2,1,0:T(8,128)(2,1)S(1)} %get-tuple-element.58.rest_0_), channel_id=1, source_target_pairs={{0,8},{4,12},{8,0},{12,4},{1,9},{5,13},{9,1},{13,5},{2,10},{6,14},... | collective-permute-start | bytes 786440 | tf_op jit(solution)/shard_map/ppermute | solution.py:500
  18.0 1.3 collective-permute-start.3
  20.2 16.1 %left.2 = (bf16[8,4,8,256,128]{4,3,2,1,0:T(8,128)(2,1)}, f32[8,128]{1,0:T(8,128)S(1)}, f32[8,128]{1,0:T(8,128)S(1)}) custom-call(s32[4]{0:T(128)S(1)} %pad_add_fusion.meta, s32[32]{0:T(128)S(1)} %copy-done.2, s32[8,2]{1,0:T(8,128)S(1)} %copy.68.partners, s32[8]{0:T(128)S(1)} %copy-done.3, bf16[8,2,16,128,128]{4,3,2,1,0:T(8,128)(2,1)} %psi_ref.13, ...), custom_call_target="tpu_custom_call" | custom-call | flops 805306368 | bytes 2621440 | tf_op jit(solution)/shard_map/left/pallas_call | solution.py:141
  37.6 2.6 %collective-permute-start.6 = (bf16[8,1,128,128]{3,2,1,0:T(8,128)(2,1)S(1)}, bf16[8,1,128,128]{3,2,1,0:T(8,128)(2,1)S(1)}, u32[]{:S(2)}, u32[]{:S(2)}) collective-permute-start(bf16[8,1,128,128]{3,2,1,0:T(8,128)(2,1)S(1)} %get-tuple-element.32.rest_0_), channel_id=1, source_target_pairs={{0,12},{4,0},{8,4},{12,8},{1,13},{5,1},{9,5},{13,9},{2,14},{6,2},{... | collective-permute-start | bytes 786440 | tf_op jit(solution)/shard_map/ppermute | solution.py:500
  40.1 13.6 %collective-permute-done.2.rest_2_ = bf16[8,1,128,128]{3,2,1,0:T(8,128)(2,1)S(1)} collective-permute-done((bf16[8,1,128,128]{3,2,1,0:T(8,128)(2,1)S(1)}, bf16[8,1,128,128]{3,2,1,0:T(8,128)(2,1)S(1)}, u32[]{:S(2)}, u32[]{:S(2)}) %collective-permute-start.2) | collective-permute-done | bytes 262176 | tf_op jit(solution)/shard_map/ppermute | solution.py:500
  53.7 1.2 choose.4
  55.1 16.0 %left.3 = (bf16[8,4,8,256,128]{4,3,2,1,0:T(8,128)(2,1)}, f32[8,128]{1,0:T(8,128)S(1)}) custom-call(s32[4]{0:T(128)S(1)} %pad_add_fusion.meta, s32[32]{0:T(128)S(1)} %copy-done.2, s32[8,2]{1,0:T(8,128)S(1)} %copy.68.partners, s32[8]{0:T(128)S(1)} %copy-done.3, bf16[8,2,16,128,128]{4,3,2,1,0:T(8,128)(2,1)} %psi_ref.13, ...), custom_call_target="tpu_custom_call" | custom-call | flops 805306368 | bytes 2621440 | tf_op jit(solution)/shard_map/left/pallas_call | solution.py:141
  71.2 3.5 %collective-permute-done.5.rest_2_ = bf16[8,1,128,128]{3,2,1,0:T(8,128)(2,1)S(1)} collective-permute-done((bf16[8,1,128,128]{3,2,1,0:T(8,128)(2,1)S(1)}, bf16[8,1,128,128]{3,2,1,0:T(8,128)(2,1)S(1)}, u32[]{:S(2)}, u32[]{:S(2)}) %collective-permute-start.5) | collective-permute-done | bytes 262176 | tf_op jit(solution)/shard_map/ppermute | solution.py:500
  74.7 1.2 choose.5
  76.0 1.6 collective-permute-start.9
  77.6 1.4 collective-permute-start.14
  79.1 12.7 %collective-permute-start.10 = (bf16[8,1,128,128]{3,2,1,0:T(8,128)(2,1)S(1)}, bf16[8,1,128,128]{3,2,1,0:T(8,128)(2,1)S(1)}, u32[]{:S(2)}, u32[]{:S(2)}) collective-permute-start(bf16[8,1,128,128]{3,2,1,0:T(8,128)(2,1)S(1)} %get-tuple-element.39.rest_0_), channel_id=1, source_target_pairs={{0,4},{4,8},{8,12},{12,0},{1,5},{5,9},{9,13},{13,1},{2,6},{6,10},{... | collective-permute-start | bytes 786440 | tf_op jit(solution)/shard_map/ppermute | solution.py:500
  91.8 1.2 collective-permute-done.9.rest_8_.rest_9_
  93.0 6.6 %collective-permute-start.12 = (bf16[8,1,128,128]{3,2,1,0:T(8,128)(2,1)S(1)}, bf16[8,1,128,128]{3,2,1,0:T(8,128)(2,1)S(1)}, u32[]{:S(2)}, u32[]{:S(2)}) collective-permute-start(bf16[8,1,128,128]{3,2,1,0:T(8,128)(2,1)S(1)} %get-tuple-element.39.rest_0_), channel_id=1, source_target_pairs={{0,12},{4,0},{8,4},{12,8},{1,13},{5,1},{9,5},{13,9},{2,14},{6,2},{... | collective-permute-start | bytes 786440 | tf_op jit(solution)/shard_map/ppermute | solution.py:500
  99.6 18.8 %chunk.4 = (f32[8,16,128,128]{3,2,1,0:T(8,128)}, f32[8,128]{1,0:T(8,128)S(1)}) custom-call(s32[4]{0:T(128)S(1)} %pad_add_fusion.meta, s32[32]{0:T(128)S(1)} %copy-done.2, s32[8,2]{1,0:T(8,128)S(1)} %copy.68.partners, s32[8]{0:T(128)S(1)} %copy-done.3, f32[8,128]{1,0:T(8,128)S(1)} %get-tuple-element.33.after_ref, bf16[8,2,16,128,128]{4,3,2,1,0:T(8,128)(2,1)} %psi_ref.13, ...), custom_call_target="tpu_custom_call" | custom-call | flops 671088640 | bytes 3670016 | tf_op jit(solution)/shard_map/chunk/pallas_call | solution.py:368
  118.4 1.4 choose.6
  119.9 19.5 %chunk.5 = (f32[8,16,128,128]{3,2,1,0:T(8,128)}, f32[8,128]{1,0:T(8,128)S(1)}) custom-call(s32[4]{0:T(128)S(1)} %pad_add_fusion.meta, s32[32]{0:T(128)S(1)} %copy-done.2, s32[8,2]{1,0:T(8,128)S(1)} %copy.68.partners, s32[8]{0:T(128)S(1)} %copy-done.3, f32[8,128]{1,0:T(8,128)S(1)} %get-tuple-element.40.after_ref, ...), custom_call_target="tpu_custom_call", output_to_operand_aliasing={{0}: (16, {})} | custom-call | flops 671088640 | bytes 3670016 | tf_op jit(solution)/shard_map/chunk/pallas_call | solution.py:368
  139.4 1.2 copy-done.1
  142.0 1.8 collective-permute-start.16
  143.9 1.1 collective-permute-start.18
  145.0 11.8 %collective-permute-done.16.rest_8_.rest_9_ = bf16[2,8,1,128,128]{4,3,2,1,0:T(8,128)(2,1)S(1)} collective-permute-done((bf16[2,8,1,128,128]{4,3,2,1,0:T(8,128)(2,1)S(1)}, bf16[2,8,1,128,128]{4,3,2,1,0:T(8,128)(2,1)S(1)}, u32[]{:S(2)}, u32[]{:S(2)}) %collective-permute-start.16) | collective-permute-done | bytes 524320 | tf_op jit(solution)/shard_map/ppermute | solution.py:468
  156.8 19.5 %chunk.6 = (f32[8,16,128,128]{3,2,1,0:T(8,128)}, f32[8,128]{1,0:T(8,128)S(1)}) custom-call(s32[4]{0:T(128)S(1)} %pad_add_fusion.meta, s32[32]{0:T(128)S(1)} %copy-done.2, s32[8,2]{1,0:T(8,128)S(1)} %copy.68.partners, s32[8]{0:T(128)S(1)} %copy-done.3, f32[8,128]{1,0:T(8,128)S(1)} %get-tuple-element.45.after_ref, ...), custom_call_target="tpu_custom_call", output_to_operand_aliasing={{0}: (16, {})} | custom-call | flops 671088640 | bytes 3670016 | tf_op jit(solution)/shard_map/chunk/pallas_call | solution.py:368
  176.3 20.7 %chunk.7 = (bf16[8,16,128,128]{3,2,1,0:T(8,128)(2,1)}, f32[8,128]{1,0:T(8,128)S(1)}) custom-call(s32[4]{0:T(128)S(1)} %pad_add_fusion.meta, s32[32]{0:T(128)S(1)} %copy-done.2, s32[8,2]{1,0:T(8,128)S(1)} %copy.68.partners, s32[8]{0:T(128)S(1)} %copy-done.3, f32[8,128]{1,0:T(8,128)S(1)} %get-tuple-element.49.after_ref, ...), custom_call_target="tpu_custom_call" | custom-call | flops 671088640 | bytes 3670016 | tf_op jit(solution)/shard_map/chunk/pallas_call | solution.py:368
  197.6 5.4 %collective-permute-done.19 = f32[16,128]{1,0:T(8,128)S(1)} collective-permute-done((f32[16,128]{1,0:T(8,128)S(1)}, f32[16,128]{1,0:T(8,128)S(1)}, u32[]{:S(2)}, u32[]{:S(2)}) %collective-permute-start.19) | collective-permute-done | bytes 8224 | tf_op jit(solution)/shard_map/ppermute | solution.py:468
  203.0 9.1 %collective-permute-start.20 = (f32[16,128]{1,0:T(8,128)S(1)}, f32[16,128]{1,0:T(8,128)S(1)}, u32[]{:S(2)}, u32[]{:S(2)}) collective-permute-start(f32[16,128]{1,0:T(8,128)S(1)} %add.24), channel_id=1, source_target_pairs={{0,4},{4,0},{8,12},{12,8},{1,5},{5,1},{9,13},{13,9},{2,6},{6,2},{1... | collective-permute-start | bytes 24584 | tf_op jit(solution)/shard_map/ppermute | solution.py:468
  212.1 1.6 collective-permute-done.20
  213.7 4.6 %collective-permute-start.21 = (f32[16,128]{1,0:T(8,128)S(1)}, f32[16,128]{1,0:T(8,128)S(1)}, u32[]{:S(2)}, u32[]{:S(2)}) collective-permute-start(f32[16,128]{1,0:T(8,128)S(1)} %add.25), channel_id=1, source_target_pairs={{0,8},{4,12},{8,0},{12,4},{1,9},{5,13},{9,1},{13,5},{2,10},{6,14},... | collective-permute-start | bytes 24584 | tf_op jit(solution)/shard_map/ppermute | solution.py:468
  218.3 1.7 collective-permute-done.21
  220.0 2.2 copy-done
  222.2 10.1 %residual.1 = (bf16[8,2,16,128,128]{4,3,2,1,0:T(8,128)(2,1)}, f32[1]{0:T(128)}) custom-call(s32[4]{0:T(128)S(1)} %pad_add_fusion.meta, s32[32]{0:T(128)S(1)} %copy-done.2, s32[8,2]{1,0:T(8,128)S(1)} %copy.68.partners, s32[8]{0:T(128)S(1)} %copy-done.3, f32[16,128]{1,0:T(8,128)S(1)} %add.26.folds_ref, bf16[8,2,16,128,128]{4,3,2,1,0:T(8,128)(2,1)S(1)} %bitcast.27, ...), custom_call_target="tpu_custom_call" | custom-call | flops 12582912 | bytes 25165824 | tf_op jit(solution)/shard_map/residual/pallas_call | solution.py:429
  (63 shorter events, 8.3 us)
Async XLA Ops:
  7.2 132.2 %all-gather.2.cloned.1.call-start = ((), (), s32[]{:S(2)}) async-start(), calls=%async_computation | async-start | bytes 1310720 | tf_op jit(solution)/shard_map/all_gather | solution.py:495
  10.2 1.4 copy-start.4
  11.1 8.2 %copy-start.5 = (s32[8,2]{0,1:T(2,128)S(1)}, s32[8,2]{0,1:T(2,128)}, u32[]{:S(2)}) copy-start(s32[8,2]{0,1:T(2,128)} %param.14) | copy-start | bytes 196
  11.1 8.4 %collective-permute-start = (bf16[2112,128]{1,0:T(8,128)(2,1)}, bf16[2112,128]{1,0:T(8,128)(2,1)S(1)}, u32[]{:S(2)}, u32[]{:S(2)}) collective-permute-start(bf16[2112,128]{1,0:T(8,128)(2,1)} %get-tuple-element.64), channel_id=1, source_target_pairs={{0,1},{1,0},{2,3},{3,2},{4,5},{5,4},{6,7},{7,6},{8,9},{9,8},{10,11... | collective-permute-start | bytes 1622024 | tf_op jit(solution)/shard_map/ppermute | solution.py:468
  12.4 25.2 %collective-permute-start.1 = (bf16[8,1,128,128]{3,2,1,0:T(8,128)(2,1)S(1)}, bf16[8,1,128,128]{3,2,1,0:T(8,128)(2,1)S(1)}, u32[]{:S(2)}, u32[]{:S(2)}) collective-permute-start(bf16[8,1,128,128]{3,2,1,0:T(8,128)(2,1)S(1)} %get-tuple-element.58.rest_0_), channel_id=1, source_target_pairs={{0,4},{4,8},{8,12},{12,0},{1,5},{5,9},{9,13},{13,1},{2,6},{6,10},{... | collective-permute-start | bytes 786440 | tf_op jit(solution)/shard_map/ppermute | solution.py:500
  15.4 38.3 %collective-permute-start.2 = (bf16[8,1,128,128]{3,2,1,0:T(8,128)(2,1)S(1)}, bf16[8,1,128,128]{3,2,1,0:T(8,128)(2,1)S(1)}, u32[]{:S(2)}, u32[]{:S(2)}) collective-permute-start(bf16[8,1,128,128]{3,2,1,0:T(8,128)(2,1)S(1)} %get-tuple-element.58.rest_0_), channel_id=1, source_target_pairs={{0,8},{4,12},{8,0},{12,4},{1,9},{5,13},{9,1},{13,5},{2,10},{6,14},... | collective-permute-start | bytes 786440 | tf_op jit(solution)/shard_map/ppermute | solution.py:500
  18.0 35.8 %collective-permute-start.3 = (bf16[8,1,128,128]{3,2,1,0:T(8,128)(2,1)S(1)}, bf16[8,1,128,128]{3,2,1,0:T(8,128)(2,1)S(1)}, u32[]{:S(2)}, u32[]{:S(2)}) collective-permute-start(bf16[8,1,128,128]{3,2,1,0:T(8,128)(2,1)S(1)} %get-tuple-element.58.rest_0_), channel_id=1, source_target_pairs={{0,12},{4,0},{8,4},{12,8},{1,13},{5,1},{9,5},{13,9},{2,14},{6,2},{... | collective-permute-start | bytes 786440 | tf_op jit(solution)/shard_map/ppermute | solution.py:500
  19.5 0.7 copy-start.2
  19.5 0.7 copy-start.3
  36.3 34.9 %collective-permute-start.4 = (bf16[8,1,128,128]{3,2,1,0:T(8,128)(2,1)S(1)}, bf16[8,1,128,128]{3,2,1,0:T(8,128)(2,1)S(1)}, u32[]{:S(2)}, u32[]{:S(2)}) collective-permute-start(bf16[8,1,128,128]{3,2,1,0:T(8,128)(2,1)S(1)} %get-tuple-element.32.rest_0_), channel_id=1, source_target_pairs={{0,4},{4,8},{8,12},{12,0},{1,5},{5,9},{9,13},{13,1},{2,6},{6,10},{... | collective-permute-start | bytes 786440 | tf_op jit(solution)/shard_map/ppermute | solution.py:500
  36.6 38.0 %collective-permute-start.5 = (bf16[8,1,128,128]{3,2,1,0:T(8,128)(2,1)S(1)}, bf16[8,1,128,128]{3,2,1,0:T(8,128)(2,1)S(1)}, u32[]{:S(2)}, u32[]{:S(2)}) collective-permute-start(bf16[8,1,128,128]{3,2,1,0:T(8,128)(2,1)S(1)} %get-tuple-element.32.rest_0_), channel_id=1, source_target_pairs={{0,8},{4,12},{8,0},{12,4},{1,9},{5,13},{9,1},{13,5},{2,10},{6,14},... | collective-permute-start | bytes 786440 | tf_op jit(solution)/shard_map/ppermute | solution.py:500
  37.6 37.1 %collective-permute-start.6 = (bf16[8,1,128,128]{3,2,1,0:T(8,128)(2,1)S(1)}, bf16[8,1,128,128]{3,2,1,0:T(8,128)(2,1)S(1)}, u32[]{:S(2)}, u32[]{:S(2)}) collective-permute-start(bf16[8,1,128,128]{3,2,1,0:T(8,128)(2,1)S(1)} %get-tuple-element.32.rest_0_), channel_id=1, source_target_pairs={{0,12},{4,0},{8,4},{12,8},{1,13},{5,1},{9,5},{13,9},{2,14},{6,2},{... | collective-permute-start | bytes 786440 | tf_op jit(solution)/shard_map/ppermute | solution.py:500
  55.0 21.0 %collective-permute-start.8 = (bf16[8,1,128,128]{3,2,0,1:T(8,128)(2,1)S(1)}, bf16[8,1,128,128]{3,2,0,1:T(8,128)(2,1)S(1)}, u32[]{:S(2)}, u32[]{:S(2)}) collective-permute-start(bf16[8,1,128,128]{3,2,0,1:T(8,128)(2,1)S(1)} %bitcast.41), channel_id=1, source_target_pairs={{0,1},{1,0},{2,3},{3,2},{4,5},{5,4},{6,7},{7,6},{8,9},{9,8},{10,11... | collective-permute-start | bytes 786440 | tf_op jit(solution)/shard_map/ppermute | solution.py:468
  55.0 44.6 %collective-permute-start.7 = (bf16[2,2112,128]{2,1,0:T(8,128)(2,1)S(1)}, bf16[2,2112,128]{2,1,0:T(8,128)(2,1)S(1)}, u32[]{:S(2)}, u32[]{:S(2)}) collective-permute-start(bf16[2,2112,128]{2,1,0:T(8,128)(2,1)S(1)} %pad_maximum_fusion.after_ref), channel_id=1, source_target_pairs={{0,2},{1,3},{2,0},{3,1},{4,6},{5,7},{6,4},{7,5},{8,10},{9,11},{10,... | collective-permute-start | bytes 3244040 | tf_op jit(solution)/shard_map/ppermute | solution.py:468
  75.9 1.7 collective-permute-start.13
  76.0 17.0 %collective-permute-start.9 = (bf16[2,8,1,128,128]{4,3,2,1,0:T(8,128)(2,1)S(1)}, bf16[2,8,1,128,128]{4,3,2,1,0:T(8,128)(2,1)S(1)}, u32[]{:S(2)}, u32[]{:S(2)}) collective-permute-start(bf16[2,8,1,128,128]{4,3,2,1,0:T(8,128)(2,1)S(1)} %pad_maximum_fusion.3), channel_id=1, source_target_pairs={{0,2},{1,3},{2,0},{3,1},{4,6},{5,7},{6,4},{7,5},{8,10},{9,11},{10,... | collective-permute-start | bytes 1572872 | tf_op jit(solution)/shard_map/ppermute | solution.py:468
  77.6 42.3 %collective-permute-start.14 = (bf16[2,8,1,128,128]{4,3,2,1,0:T(8,128)(2,1)S(1)}, bf16[2,8,1,128,128]{4,3,2,1,0:T(8,128)(2,1)S(1)}, u32[]{:S(2)}, u32[]{:S(2)}) collective-permute-start(bf16[2,8,1,128,128]{4,3,2,1,0:T(8,128)(2,1)S(1)} %pad_maximum_fusion.4), channel_id=1, source_target_pairs={{0,2},{1,3},{2,0},{3,1},{4,6},{5,7},{6,4},{7,5},{8,10},{9,11},{10,... | collective-permute-start | bytes 1572872 | tf_op jit(solution)/shard_map/ppermute | solution.py:468
  79.1 39.3 %collective-permute-start.10 = (bf16[8,1,128,128]{3,2,1,0:T(8,128)(2,1)S(1)}, bf16[8,1,128,128]{3,2,1,0:T(8,128)(2,1)S(1)}, u32[]{:S(2)}, u32[]{:S(2)}) collective-permute-start(bf16[8,1,128,128]{3,2,1,0:T(8,128)(2,1)S(1)} %get-tuple-element.39.rest_0_), channel_id=1, source_target_pairs={{0,4},{4,8},{8,12},{12,0},{1,5},{5,9},{9,13},{13,1},{2,6},{6,10},{... | collective-permute-start | bytes 786440 | tf_op jit(solution)/shard_map/ppermute | solution.py:500
  91.8 26.7 %collective-permute-start.11 = (bf16[8,1,128,128]{3,2,1,0:T(8,128)(2,1)S(1)}, bf16[8,1,128,128]{3,2,1,0:T(8,128)(2,1)S(1)}, u32[]{:S(2)}, u32[]{:S(2)}) collective-permute-start(bf16[8,1,128,128]{3,2,1,0:T(8,128)(2,1)S(1)} %get-tuple-element.39.rest_0_), channel_id=1, source_target_pairs={{0,8},{4,12},{8,0},{12,4},{1,9},{5,13},{9,1},{13,5},{2,10},{6,14},... | collective-permute-start | bytes 786440 | tf_op jit(solution)/shard_map/ppermute | solution.py:500
  93.0 25.4 %collective-permute-start.12 = (bf16[8,1,128,128]{3,2,1,0:T(8,128)(2,1)S(1)}, bf16[8,1,128,128]{3,2,1,0:T(8,128)(2,1)S(1)}, u32[]{:S(2)}, u32[]{:S(2)}) collective-permute-start(bf16[8,1,128,128]{3,2,1,0:T(8,128)(2,1)S(1)} %get-tuple-element.39.rest_0_), channel_id=1, source_target_pairs={{0,12},{4,0},{8,4},{12,8},{1,13},{5,1},{9,5},{13,9},{2,14},{6,2},{... | collective-permute-start | bytes 786440 | tf_op jit(solution)/shard_map/ppermute | solution.py:500
  119.8 22.1 %collective-permute-start.15 = (bf16[8,1,128,128]{3,2,0,1:T(8,128)(2,1)S(1)}, bf16[8,1,128,128]{3,2,0,1:T(8,128)(2,1)S(1)}, u32[]{:S(2)}, u32[]{:S(2)}) collective-permute-start(bf16[8,1,128,128]{3,2,0,1:T(8,128)(2,1)S(1)} %bitcast.42), channel_id=1, source_target_pairs={{0,1},{1,0},{2,3},{3,2},{4,5},{5,4},{6,7},{7,6},{8,9},{9,8},{10,11... | collective-permute-start | bytes 786440 | tf_op jit(solution)/shard_map/ppermute | solution.py:468
  139.4 1.2 copy-start.1
  141.3 2.6 %collective-permute-start.17 = (bf16[8,1,128,128]{3,2,0,1:T(8,128)(2,1)S(1)}, bf16[8,1,128,128]{3,2,0,1:T(8,128)(2,1)S(1)}, u32[]{:S(2)}, u32[]{:S(2)}) collective-permute-start(bf16[8,1,128,128]{3,2,0,1:T(8,128)(2,1)S(1)} %bitcast.44), channel_id=1, source_target_pairs={{0,1},{1,0},{2,3},{3,2},{4,5},{5,4},{6,7},{7,6},{8,9},{9,8},{10,11... | collective-permute-start | bytes 786440 | tf_op jit(solution)/shard_map/ppermute | solution.py:468
  142.0 14.8 %collective-permute-start.16 = (bf16[2,8,1,128,128]{4,3,2,1,0:T(8,128)(2,1)S(1)}, bf16[2,8,1,128,128]{4,3,2,1,0:T(8,128)(2,1)S(1)}, u32[]{:S(2)}, u32[]{:S(2)}) collective-permute-start(bf16[2,8,1,128,128]{4,3,2,1,0:T(8,128)(2,1)S(1)} %pad_maximum_fusion.5), channel_id=1, source_target_pairs={{0,2},{1,3},{2,0},{3,1},{4,6},{5,7},{6,4},{7,5},{8,10},{9,11},{10,... | collective-permute-start | bytes 1572872 | tf_op jit(solution)/shard_map/ppermute | solution.py:468
  143.9 32.4 %collective-permute-start.18 = (bf16[2,8,1,128,128]{4,3,2,1,0:T(8,128)(2,1)S(1)}, bf16[2,8,1,128,128]{4,3,2,1,0:T(8,128)(2,1)S(1)}, u32[]{:S(2)}, u32[]{:S(2)}) collective-permute-start(bf16[2,8,1,128,128]{4,3,2,1,0:T(8,128)(2,1)S(1)} %pad_maximum_fusion.6), channel_id=1, source_target_pairs={{0,2},{1,3},{2,0},{3,1},{4,6},{5,7},{6,4},{7,5},{8,10},{9,11},{10,... | collective-permute-start | bytes 1572872 | tf_op jit(solution)/shard_map/ppermute | solution.py:468
  176.3 43.7 %slice-start = ((s8[8388608]{0:T(1024)(128)(4,1)}), s8[4194304]{0:T(1024)(128)(4,1)S(1)}, s32[]{:S(2)}) async-start(s8[8388608]{0:T(1024)(128)(4,1)} %bitcast.26), calls=%async_computation.1 | async-start | bytes 8388608
  176.3 43.7 %slice-start.1 = ((s8[8388608]{0:T(1024)(128)(4,1)}), s8[4194304]{0:T(1024)(128)(4,1)S(1)}, s32[]{:S(2)}) async-start(s8[8388608]{0:T(1024)(128)(4,1)} %bitcast.26), calls=%async_computation.2 | async-start | bytes 8388608
  197.1 22.9 %collective-permute-start.22 = (bf16[8,16,128,128]{3,2,1,0:T(8,128)(2,1)}, bf16[8,16,128,128]{3,2,1,0:T(8,128)(2,1)S(1)}, u32[]{:S(2)}, u32[]{:S(2)}) collective-permute-start(bf16[8,16,128,128]{3,2,1,0:T(8,128)(2,1)} %get-tuple-element.55.own_ref), channel_id=1, source_target_pairs={{0,1},{1,0},{2,3},{3,2},{4,5},{5,4},{6,7},{7,6},{8,9},{9,8},{10,11... | collective-permute-start | bytes 12582920 | tf_op jit(solution)/shard_map/ppermute | solution.py:468
  197.1 5.9 %collective-permute-start.19 = (f32[16,128]{1,0:T(8,128)S(1)}, f32[16,128]{1,0:T(8,128)S(1)}, u32[]{:S(2)}, u32[]{:S(2)}) collective-permute-start(f32[16,128]{1,0:T(8,128)S(1)} %constant_dynamic-update-slice_fusion), channel_id=1, source_target_pairs={{0,1},{1,0},{2,3},{3,2},{4,5},{5,4},{6,7},{7,6},{8,9},{9,8},{10,11... | collective-permute-start | bytes 24584 | tf_op jit(solution)/shard_map/ppermute | solution.py:468
  203.0 10.7 %collective-permute-start.20 = (f32[16,128]{1,0:T(8,128)S(1)}, f32[16,128]{1,0:T(8,128)S(1)}, u32[]{:S(2)}, u32[]{:S(2)}) collective-permute-start(f32[16,128]{1,0:T(8,128)S(1)} %add.24), channel_id=1, source_target_pairs={{0,4},{4,0},{8,12},{12,8},{1,5},{5,1},{9,13},{13,9},{2,6},{6,2},{1... | collective-permute-start | bytes 24584 | tf_op jit(solution)/shard_map/ppermute | solution.py:468
  213.7 6.3 %collective-permute-start.21 = (f32[16,128]{1,0:T(8,128)S(1)}, f32[16,128]{1,0:T(8,128)S(1)}, u32[]{:S(2)}, u32[]{:S(2)}) collective-permute-start(f32[16,128]{1,0:T(8,128)S(1)} %add.25), channel_id=1, source_target_pairs={{0,8},{4,12},{8,0},{12,4},{1,9},{5,13},{9,1},{13,5},{2,10},{6,14},... | collective-permute-start | bytes 24584 | tf_op jit(solution)/shard_map/ppermute | solution.py:468
  220.0 2.2 copy-start
Sparse Core Ops, SparseCore 0:
  19.5 47.0 all-gather.1
